TPU v7x, 128 devices: a whole 4x4x4 slice. The times are simulated.
128 devices in a mesh: rows: 8 (over z, core), cols: 16 (over y, x).
Axes of the slice: x: 4, y: 4, z: 4, core: 2. Of those that a mesh axis runs over, the one named last changes fastest.
Arguments:
- row_bases: bfloat16 [32, 128, 2048], P('rows', None, 'cols'), may hold values from -6 to 6
- col_bases: bfloat16 [768, 128, 2048], P('cols', None, 'rows'), may hold values from -6 to 6
- test_matrix: bfloat16 [768, 64, 2048], P('cols', None, 'rows'), may hold values from -6 to 6
- couplings: bfloat16 [8192, 64, 128], P(('rows', 'cols')), may hold values from -6 to 6
- tile_rows: int32 [8192], P(('rows', 'cols')), may hold values from 0 to 4, as said below
- tile_cols: int32 [8192], P(('rows', 'cols')), may hold values from 0 to 767, as said below
Outputs:
- new_basis: float32 [32, 64, 2048], P('rows', None, 'cols')
- new_couplings: float32 [8192, 64, 128], P(('rows', 'cols'))
Inputs may be any that keep to these rules, and one draw needn't show every extreme that they name: `tile_rows`: the 64 slots of one device hold the tiles of block rows of its own row group only; they are 4-slot buckets in order, bucket k holding only block columns kept on cols index k; live slots of a bucket come first. In every row group some bucket index is full on every device, and every block row of the slab has live tiles. `tile_cols`: in bucket k of any device the block column lies in k * 48 to (k + 1) * 48 - 1, empty slots too.
All inputs are finite; a program needn't handle non-finite values.
Results may differ from a plain program's by a relative error of at most 0.0003.
Values may be sent and summed in bfloat16 or wider, within the bound.
A program may use at most 128 MiB of HBM per device.

v0:
```python
import math

import jax
import jax.numpy as jnp
from jax import lax
from jax.sharding import PartitionSpec as P

LEAF = 2048
BR_DEV = 4


def tile_terms(picked, couplings, weights):
    highest_precision = lax.Precision.HIGHEST
    sketch_width = couplings.shape[1]
    coupled = couplings.astype(jnp.float32)
    first_operator = jnp.einsum(
        "tak,tbk->tab",
        picked[:, :, :sketch_width],
        coupled[:, :, :sketch_width],
        precision=highest_precision,
    )
    second_operator = jnp.einsum(
        "tak,tbk->tab",
        picked[:, :, sketch_width:],
        coupled[:, :, sketch_width:],
        precision=highest_precision,
    )
    terms = jnp.concatenate([first_operator, second_operator], axis=2)
    return jnp.einsum("ti,tab->iab", weights, terms, precision=highest_precision)


def local(row_bases, col_bases, test_matrix, couplings, tile_rows, tile_cols):
    highest_precision = lax.Precision.HIGHEST
    sketch_width = test_matrix.shape[1]
    partial_sketch = jnp.einsum(
        "jal,jkl->jak", test_matrix, col_bases, preferred_element_type=jnp.float32
    ) / math.sqrt(LEAF)
    sketch = lax.psum(partial_sketch, "rows")
    blocks = jnp.arange(BR_DEV, dtype=jnp.int32)
    own_weights = (tile_rows[:, None] == blocks[None, :]).astype(jnp.float32)
    piece = lax.all_gather(sketch, "cols", axis=0, tiled=True)
    count = piece.shape[0]
    inside = ((tile_cols >= 0) & (tile_cols < count)).astype(jnp.float32)
    picked = jnp.take(piece, jnp.clip(tile_cols, 0, count - 1), axis=0)
    sketch_part = tile_terms(picked, couplings, own_weights * inside[:, None])
    gram_part = (
        jnp.einsum("ikl,iml->ikm", row_bases, row_bases, preferred_element_type=jnp.float32) / LEAF
    )
    row_side_sketch, gram = lax.psum((sketch_part, gram_part), "cols")
    middle_factor = jnp.einsum("iab,ibc->iac", row_side_sketch, gram, precision=highest_precision)
    curvature_factor = jnp.einsum(
        "jgy,jsy->jgs", middle_factor, row_side_sketch, precision=highest_precision
    )
    lower = jnp.linalg.cholesky(curvature_factor)
    coeff = jax.vmap(lambda a, b: jax.scipy.linalg.solve_triangular(a, b, lower=True))(
        lower, row_side_sketch
    )
    new_basis = jnp.einsum(
        "iak,ikl->ial", coeff, row_bases.astype(jnp.float32), precision=highest_precision
    )
    projected = jnp.einsum("iab,ibc->iac", coeff, gram, precision=highest_precision)
    selected_columns = jnp.einsum(
        "ti,iab->tab", own_weights, projected, precision=highest_precision
    )
    coupled_matrix = couplings.astype(jnp.float32)
    first_operator = jnp.einsum(
        "zdp,zpv->zdv",
        selected_columns[:, :, :sketch_width],
        coupled_matrix[:, :, :sketch_width],
        precision=highest_precision,
    )
    second_operator = jnp.einsum(
        "zdp,zpv->zdv",
        selected_columns[:, :, sketch_width:],
        coupled_matrix[:, :, sketch_width:],
        precision=highest_precision,
    )
    new_couplings = jnp.concatenate([first_operator, second_operator], axis=2)
    return (new_basis, new_couplings)


def solution(mesh):
    in_specs = (
        P("rows", None, "cols"),
        P("cols", None, "rows"),
        P("cols", None, "rows"),
        P(("rows", "cols"), None, None),
        P(("rows", "cols")),
        P(("rows", "cols")),
    )
    out_specs = (P("rows", None, "cols"), P(("rows", "cols"), None, None))
    return jax.shard_map(local, mesh=mesh, in_specs=in_specs, out_specs=out_specs, check_vma=False)
```

profile of v0, /device:TPU:0, one launch (start us, length us, event | category | flops | bytes accessed | tf_op | source)
XLA Modules:
  0.0 406.1 jit_solution(11924850720004038013)
XLA Ops:
  7.2 0.0 copy-start
  7.2 0.0 all-reduce.4.cloned.1.call-start
  7.2 1.8 copy-done
  9.1 3.8 convolution_multiply_fusion
  12.8 0.0 copy-start.5
  12.8 0.0 copy-start.3
  12.8 0.0 all-reduce.4.cloned.1.call-update
  12.8 0.0 all-gather.2.cloned.1.call-start
  12.9 66.9 %all-reduce.4.cloned.1.call-done = f32[48,64,128]{2,1,0:T(8,128)} async-done(((f32[48,64,128]{2,1,0:T(8,128)}), f32[48,64,128]{2,1,0:T(8,128)}) %all-reduce.4.cloned.1.call-update) | async-done | bytes 1572880 | tf_op jit(solution)/shard_map/psum | solution.py:38
  79.8 0.0 all-gather.2.cloned.1.call-update
  79.8 0.0 all-reduce.6.cloned.1.call-start
  79.8 0.0 copy-done.5
  79.9 0.0 copy-done.3
  79.9 0.9 convolution_multiply_fusion.1
  80.8 154.5 %all-gather.2.cloned.1.call-done = f32[768,64,128]{2,1,0:T(8,128)} async-done(((f32[48,64,128]{2,1,0:T(8,128)}), f32[768,64,128]{2,1,0:T(8,128)}) %all-gather.2.cloned.1.call-update) | async-done | bytes 25165840 | tf_op jit(solution)/shard_map/all_gather | solution.py:41
  235.3 10.2 %gather_fusion = f32[64,64,128]{2,1,0:T(8,128)} fusion(f32[768,64,128]{2,1,0:T(8,128)} %all-gather.2.cloned.1.call-done, s32[1024]{0:T(1024)S(1)} %pad_clamp_fusion), kind=kCustom, calls=%fused_computation | custom fusion | bytes 4194560 | tf_op jit(solution)/shard_map/jit(_take)/gather | solution.py:44
  245.4 0.0 copy-start.1
  245.4 1.9 broadcast_select_fusion
  247.3 0.0 copy-done.1
  247.3 2.1 fusion
  249.5 1.8 fusion.2
  251.3 0.0 copy-start.4
  251.3 0.6 pad_maximum_fusion
  251.9 0.0 copy-done.4
  251.9 2.9 fusion.8
  254.8 0.0 all-reduce.6.cloned.1.call-update
  254.9 84.0 %all-reduce.6.cloned.1.call-done = (f32[4,128,128]{2,1,0:T(8,128)}, f32[4,64,128]{2,0,1:T(4,128)}) async-done(((f32[4,128,128]{2,1,0:T(8,128)}, f32[4,64,128]{2,0,1:T(4,128)}), (f32[4,128,128]{2,1,0:T(8,128)}, f32[4,64,128]{2,0,1:T(4,128)})) %all-reduce.6.cloned.1.call-update) | async-done | bytes 393232 | tf_op jit(solution)/shard_map/psum | solution.py:49
  338.9 1.4 fusion.22
  340.3 1.2 fusion.20
  341.5 0.1 copy.23
  341.6 0.7 fusion.16
  342.3 24.2 %custom-call.8 = f32[4,64,64]{2,1,0:T(8,128)S(1)} custom-call(f32[4,64,64]{2,1,0:T(8,128)} %fusion.16), custom_call_target="Cholesky" | custom-call | tf_op jit(solution)/shard_map/jit(cholesky)/cholesky | solution.py:54
  366.5 0.1 compare_reduce_fusion
  366.7 0.1 select_bitcast_fusion
  366.8 19.7 %custom-call.9 = f32[4,1,64,64]{2,3,1,0:T(8,128)S(1)} custom-call(f32[4,1,64,64]{3,2,1,0:T(8,128)S(1)} %select_bitcast_fusion), custom_call_target="InvertDiagBlocksLowerTriangular" | custom-call | tf_op jit(solution)/shard_map/vmap(jit(_solve_triangular))/triangular_solve | solution.py:55
  386.4 1.3 fusion.14
  387.7 1.3 fusion.35
  389.0 0.9 fusion.34
  389.9 1.7 fusion.17
  391.6 0.0 copy-start.2
  391.6 0.8 fusion.33
  392.5 0.4 copy-done.2
  392.9 2.4 fusion.4
  395.3 2.4 fusion.6
  397.7 1.9 pad_maximum_fusion.1
  (5 shorter events, 0.1 us)
Async XLA Ops:
  7.2 1.9 copy-start
  7.2 72.6 %all-reduce.4.cloned.1.call-start = ((), (), s32[]{:S(2)}) async-start(), calls=%async_computation | async-start | bytes 3145728 | tf_op jit(solution)/shard_map/psum | solution.py:38
  12.8 67.0 %copy-start.5 = (s32[64]{0:T(128)S(1)}, s32[64]{0:T(128)}, u32[]{:S(2)}) copy-start(s32[64]{0:T(128)} %param.11) | copy-start | bytes 772
  12.8 67.1 %copy-start.3 = (bf16[4,128,128]{2,1,0:T(8,128)(2,1)S(1)}, bf16[4,128,128]{2,1,0:T(8,128)(2,1)}, u32[]{:S(2)}) copy-start(bf16[4,128,128]{2,1,0:T(8,128)(2,1)} %param.6) | copy-start | bytes 393220
  12.8 222.4 %all-gather.2.cloned.1.call-start = ((), (), s32[]{:S(2)}) async-start(), calls=%async_computation.1 | async-start | bytes 26738688 | tf_op jit(solution)/shard_map/all_gather | solution.py:41
  79.8 259.1 %all-reduce.6.cloned.1.call-start = ((), (), s32[]{:S(2)}) async-start(), calls=%async_computation.2 | async-start | bytes 786432 | tf_op jit(solution)/shard_map/psum | solution.py:49
  245.4 1.9 copy-start.1
  251.3 0.7 copy-start.4
  391.6 1.2 copy-start.2
Sparse Core Ops, SparseCore 0:
  13.0 66.7 all-reduce.3
  81.9 153.3 all-gather.1
  255.0 83.8 all-reduce.5
where the time goes:
time: 407 us; the launch traced here: 406 us
  waiting for transfers between devices  305 us (75%)
  other arithmetic  49.2 us (12%)
  matrix products  24.1 us (6%)
  between operations  13.9 us (3%)
  local copies, waits for them, and re-layouts  13.4 us (3%)
    all_gather x1, waiting for transfers between devices, local(): piece = lax.all_gather(sketch, 'cols', axis=0, tiled=True)  154 us
    psum x1, waiting for transfers between devices, local(): row_side_sketch, gram = lax.psum((sketch_part, gram_part), 'cols')  84 us
    psum x1, waiting for transfers between devices, local(): sketch = lax.psum(partial_sketch, 'rows')  66.9 us
    another operation x4, other arithmetic, local(): lower = jnp.linalg.cholesky(curvature_factor)  24.3 us
    another operation x3, other arithmetic, local(): jax.scipy.linalg.solve_triangular(a, b, lower=True)  19.8 us
    gather x1, local copies, waits for them, and re-layouts, local(): picked = jnp.take(piece, jnp.clip(tile_cols, 0, count - 1), axis=0)  10.2 us
  transfers between devices with their start and end apart: 3, of which 3 were waited for; matrix products, arithmetic and copies ran while one was open for 0% of the time, Pallas kernels for 0%

commit v1 on v0

v1 whole, which is shorter than its diff:
```python
import functools
import math

import jax
import jax.numpy as jnp
from jax import lax
from jax.experimental import pallas as pl
from jax.experimental.pallas import tpu as pltpu
from jax.sharding import PartitionSpec as P

MESH = pl.DeviceIdType.MESH
F32 = jnp.float32
BF16 = jnp.bfloat16
LEAF = 2048
SCALE = 1.0 / math.sqrt(LEAF)
CB = 48
HALF = 24
CH = 6
HC = 3
NCOL = 16
NT = (((1,), (1,)), ((), ()))
NN = (((1,), (0,)), ((), ()))
OFFSETS = [(dy, dx) for dy in range(4) for dx in range(4) if (dy, dx) != (0, 0)]


def split_hi_lo(value):
    hi = value.astype(BF16)
    return hi, (value - hi.astype(F32)).astype(BF16)


def front_kernel(
    cb, tm, cp, rb, idx, out_r, out_g,
    cbv, tmv, rbv, part, own, prx, zr1, zr2, full, cpl, idxv, idxs,
    gpart, grx, gall, rpart, rrx, rall,
    ld_sem, misc_sem, pc_send, pc_recv, zs_send, zs_recv, ag_send, ag_recv, fw_send, fw_recv,
    cp_send, cp_recv, ix_send, ix_recv, g1_send, g1_recv, g2_send, g2_recv,
    r1_send, r1_recv, r2_send, r2_recv,
):
    r = lax.axis_index("rows")
    k = lax.axis_index("cols")
    z, h = lax.div(r, 2), lax.rem(r, 2)
    y, x = lax.div(k, 4), lax.rem(k, 4)
    partner = (r + 1 - 2 * h, k)
    up = (lax.rem(z + 1, 4) * 2 + h, k)
    down = (lax.rem(z + 3, 4) * 2 + h, k)
    peers = [lax.rem(y + dy, 4) * 4 + lax.rem(x + dx, 4) for dy, dx in OFFSETS]

    def zc(q):
        return lax.rem(z + q, 4) * CH

    order = (2, 1, 3, 0)
    loads = {}
    for n, half in enumerate((1 - h, h)):
        for m, q in enumerate(order):
            at = pl.ds(half * HALF + zc(q), CH)
            a = pltpu.make_async_copy(cb.at[at], cbv.at[at], ld_sem.at[0, n * 4 + m])
            b = pltpu.make_async_copy(tm.at[at], tmv.at[at], ld_sem.at[1, n * 4 + m])
            a.start()
            b.start()
            loads[n, q] = (a, b)
    load_rb = pltpu.make_async_copy(rb, rbv, misc_sem.at[0])
    load_rb.start()
    own_cp = pltpu.make_async_copy(cp.at[pl.ds(4 * k, 4)], cpl.at[k], misc_sem.at[1])
    own_cp.start()
    own_ix = pltpu.make_async_copy(idx, idxv.at[k], misc_sem.at[2])
    own_ix.start()

    barrier = pltpu.get_barrier_semaphore()
    for device in [partner, up, down] + [(r, c) for c in peers]:
        pl.semaphore_signal(barrier, inc=1, device_id=device, device_id_type=MESH)

    def sketch(n, q, dst):
        for load in loads[n, q]:
            load.wait()
        half = (1 - h) if n == 0 else h
        base = half * HALF + zc(q)

        @pl.loop(0, CH, unroll=True)
        def _(u):
            dst[zc(q) + u] = (
                lax.dot_general(tmv[base + u], cbv[base + u], NT, preferred_element_type=F32) * SCALE
            )

    def remote(src, dst, send, recv, device):
        return pltpu.make_async_remote_copy(
            src_ref=src, dst_ref=dst, send_sem=send, recv_sem=recv, device_id=device, device_id_type=MESH
        )

    started = []

    def go(copy):
        copy.start()
        started.append(copy)
        return copy

    sketch(0, 2, part)
    pl.semaphore_wait(barrier, 3 + len(OFFSETS))
    to_partner = {}

    def send_partner(m, q):
        at = pl.ds(zc(q), CH)
        to_partner[q] = go(remote(part.at[at], prx.at[at], pc_send.at[m], pc_recv.at[m], partner))

    send_partner(0, 2)
    moves = []
    for n, c in enumerate(peers):
        moves.append((
            go(remote(cp.at[pl.ds(4 * c, 4)], cpl.at[k], cp_send.at[n], cp_recv.at[n], (r, c))),
            go(remote(idx, idxv.at[k], ix_send.at[n], ix_recv.at[n], (r, c))),
        ))
    for m, q in enumerate(order):
        if m:
            sketch(0, q, part)
            send_partner(m, q)

    def add_partner(q):
        sketch(1, q, own)
        to_partner[q].wait_recv()
        at = pl.ds(zc(q), CH)
        own[at] = own[at] + prx[at]

    add_partner(2)
    a2 = go(remote(own.at[pl.ds(zc(2), HC)], zr1.at[0], zs_send.at[0], zs_recv.at[0], up))
    b2 = go(remote(own.at[pl.ds(zc(2) + HC, HC)], zr1.at[1], zs_send.at[1], zs_recv.at[1], down))
    add_partner(1)
    b1 = go(remote(own.at[pl.ds(zc(1) + HC, HC)], zr2.at[1], zs_send.at[2], zs_recv.at[2], up))
    add_partner(3)
    a3 = go(remote(own.at[pl.ds(zc(3), HC)], zr2.at[2], zs_send.at[3], zs_recv.at[3], down))
    add_partner(0)

    load_rb.wait()
    for i in range(4):
        gpart[:, pl.ds(i * 128, 128)] = lax.dot_general(rbv[i], rbv[i], NT, preferred_element_type=F32) * (1.0 / LEAF)
    gram1 = [
        go(remote(gpart.at[pl.ds(8 * c, 8)], grx.at[n], g1_send.at[n], g1_recv.at[n], (r, c)))
        for n, c in enumerate(peers)
    ]

    a2.wait_recv()
    at = pl.ds(zc(1), HC)
    own[at] = own[at] + zr1[0]
    a1 = go(remote(own.at[at], zr2.at[0], zs_send.at[4], zs_recv.at[4], up))
    b2.wait_recv()
    at = pl.ds(zc(3) + HC, HC)
    own[at] = own[at] + zr1[1]
    b3 = go(remote(own.at[at], zr2.at[3], zs_send.at[5], zs_recv.at[5], down))

    for copy in gram1:
        copy.wait_recv()
    total = gpart[pl.ds(pl.multiple_of(8 * k, 8), 8)]
    for n in range(len(OFFSETS)):
        total = total + grx[n]
    gall[k] = total
    gram2 = [
        go(remote(gall.at[k], gall.at[k], g2_send.at[n], g2_recv.at[n], (r, c)))
        for n, c in enumerate(peers)
    ]

    for copy in (b1, a3, a1, b3):
        copy.wait_recv()
    mine = h * HALF + zc(0)
    at = pl.ds(zc(0), HC)
    full[pl.ds(mine, HC)] = own[at] + zr2[0] + zr2[2]
    at = pl.ds(zc(0) + HC, HC)
    full[pl.ds(mine + HC, HC)] = own[at] + zr2[1] + zr2[3]

    def spread(start, count, send, recv, device):
        at = pl.ds(start, count)
        return go(remote(full.at[at], full.at[at], send, recv, device))

    g_up = spread(mine, CH, ag_send.at[0], ag_recv.at[0], up)
    g_down = spread(mine, CH, ag_send.at[1], ag_recv.at[1], down)
    forwarded = [spread(mine, CH, fw_send.at[0], fw_recv.at[0], partner)]
    g_up.wait_recv()
    below = h * HALF + zc(3)
    f_up = spread(below, HC, ag_send.at[2], ag_recv.at[2], up)
    forwarded.append(spread(below, CH, fw_send.at[1], fw_recv.at[1], partner))
    g_down.wait_recv()
    above = h * HALF + zc(1)
    f_down = spread(above + HC, HC, ag_send.at[3], ag_recv.at[3], down)
    forwarded.append(spread(above, CH, fw_send.at[2], fw_recv.at[2], partner))
    far = h * HALF + zc(2)
    f_up.wait_recv()
    forwarded.append(spread(far, HC, fw_send.at[3], fw_recv.at[3], partner))
    f_down.wait_recv()
    forwarded.append(spread(far + HC, HC, fw_send.at[4], fw_recv.at[4], partner))

    own_cp.wait()
    own_ix.wait()
    for a, b in moves:
        a.wait_recv()
        b.wait_recv()
    to_scalars = pltpu.make_async_copy(idxv, idxs, misc_sem.at[3])
    to_scalars.start()
    to_scalars.wait()
    for copy in forwarded:
        copy.wait_recv()

    first = lax.broadcasted_iota(jnp.int32, (64, 128), 1) < 64

    def tiles(c, carry):
        sums = list(carry)
        for s in range(4):
            j = jnp.clip(idxs[c, 0, 4 * k + s] - CB * k, 0, CB - 1)
            row = idxs[c, 0, 64 + 4 * k + s]
            hi, lo = split_hi_lo(full[j])
            coupling = cpl[c, s].astype(F32)
            zero = jnp.zeros_like(coupling)
            pair = jnp.concatenate(
                [jnp.where(first, coupling, zero), jnp.where(first, zero, coupling)], axis=0
            ).astype(BF16)
            both = lax.dot_general(jnp.concatenate([hi, lo], axis=0), pair, NT, preferred_element_type=F32)
            term = both[:64] + both[64:]
            for i in range(4):
                sums[i] = sums[i] + jnp.where(row == i, 1.0, 0.0) * term
        return tuple(sums)

    sums = lax.fori_loop(0, NCOL, tiles, (jnp.zeros((64, 128), F32),) * 4)
    for i in range(4):
        rpart[pl.ds(4 * i, 4)] = sums[i].reshape(4, 16, 128)

    row1 = [
        go(remote(rpart.at[c], rrx.at[n], r1_send.at[n], r1_recv.at[n], (r, c)))
        for n, c in enumerate(peers)
    ]
    for copy in row1:
        copy.wait_recv()
    total = rpart[k]
    for n in range(len(OFFSETS)):
        total = total + rrx[n]
    rall[k] = total
    row2 = [
        go(remote(rall.at[k], rall.at[k], r2_send.at[n], r2_recv.at[n], (r, c)))
        for n, c in enumerate(peers)
    ]
    for copy in gram2:
        copy.wait_recv()
    for c in range(NCOL):
        for i in range(4):
            out_g[i, pl.ds(8 * c, 8)] = gall[c, :, pl.ds(128 * i, 128)]
    for copy in row2:
        copy.wait_recv()
    out_r[...] = rall[...]
    for copy in started:
        copy.wait_send()


def front(cb, tm, cp, rb, idx):
    any_space = pl.BlockSpec(memory_space=pl.ANY)
    vmem = pl.BlockSpec(memory_space=pltpu.VMEM)
    dma = pltpu.SemaphoreType.DMA
    peers = len(OFFSETS)
    return pl.pallas_call(
        front_kernel,
        out_shape=(
            jax.ShapeDtypeStruct((NCOL, 16, 128), F32),
            jax.ShapeDtypeStruct((4, 128, 128), F32),
        ),
        in_specs=[any_space] * 5,
        out_specs=(vmem, vmem),
        scratch_shapes=[
            pltpu.VMEM((CB, 128, 256), BF16),
            pltpu.VMEM((CB, 64, 256), BF16),
            pltpu.VMEM((4, 128, 128), BF16),
            pltpu.VMEM((HALF, 64, 128), F32),
            pltpu.VMEM((HALF, 64, 128), F32),
            pltpu.VMEM((HALF, 64, 128), F32),
            pltpu.VMEM((2, HC, 64, 128), F32),
            pltpu.VMEM((4, HC, 64, 128), F32),
            pltpu.VMEM((CB, 64, 128), F32),
            pltpu.VMEM((NCOL, 4, 64, 128), BF16),
            pltpu.VMEM((NCOL, 8, 128), jnp.int32),
            pltpu.SMEM((NCOL, 8, 128), jnp.int32),
            pltpu.VMEM((128, 512), F32),
            pltpu.VMEM((peers, 8, 512), F32),
            pltpu.VMEM((NCOL, 8, 512), F32),
            pltpu.VMEM((NCOL, 16, 128), F32),
            pltpu.VMEM((peers, 16, 128), F32),
            pltpu.VMEM((NCOL, 16, 128), F32),
            dma((2, 8)), dma((4,)),
            dma((4,)), dma((4,)), dma((6,)), dma((6,)), dma((4,)), dma((4,)), dma((5,)), dma((5,)),
        ] + [dma((peers,))] * 12,
        compiler_params=pltpu.CompilerParams(
            collective_id=0, has_side_effects=True, vmem_limit_bytes=40 * 1024 * 1024
        ),
    )(cb, tm, cp, rb, idx)


def back_kernel(rows_s, r_ref, g_ref, rb, cp, nb, nc, cpv, rbv, ncv, proj, sem, out_sem):
    load_cp = pltpu.make_async_copy(cp, cpv, sem.at[0])
    load_cp.start()
    load_rb = pltpu.make_async_copy(rb, rbv, sem.at[1])
    load_rb.start()
    highest = lax.Precision.HIGHEST

    work_a, work_r = [], []
    for i in range(4):
        rs = r_ref[pl.ds(4 * i, 4)].reshape(64, 128)
        middle = lax.dot_general(rs, g_ref[i], NN, precision=highest, preferred_element_type=F32)
        a = lax.dot_general(middle, rs, NT, precision=highest, preferred_element_type=F32)
        work_a.append([a[8 * b:8 * b + 8] for b in range(8)])
        work_r.append([rs[8 * b:8 * b + 8] for b in range(8)])

    sub = lax.broadcasted_iota(jnp.int32, (8, 128), 0)
    for step in range(16):
        b, o = divmod(4 * step, 8)
        for i in range(4):
            a, rr = work_a[i], work_r[i]
            cols = [
                [jnp.broadcast_to(a[n][:, 4 * step + p:4 * step + p + 1], (8, 128)) for n in range(b, 8)]
                for p in range(4)
            ]
            ra = [a[b][o + p:o + p + 1] for p in range(4)]
            rw = [rr[b][o + p:o + p + 1] for p in range(4)]
            mult, ua, ur = [], [], []
            for p in range(4):
                col, va, vr = cols[p], ra[p], rw[p]
                for q in range(p):
                    l = mult[q][0][o + p:o + p + 1]
                    col = [cc - mm * l for cc, mm in zip(col, mult[q])]
                    va = va - l[:, :64] * ua[q]
                    vr = vr - l * ur[q]
                inv = lax.rsqrt(col[0][o + p:o + p + 1])
                mult.append([cc * inv for cc in col])
                ua.append(va * inv[:, :64])
                ur.append(vr * inv)
            below = sub >= o + 4
            for n in range(b, 8):
                if n == b and o == 4:
                    continue
                da = sum(mult[p][n - b][:, :64] * ua[p] for p in range(4))
                dr = sum(mult[p][n - b] * ur[p] for p in range(4))
                if n == b:
                    da = jnp.where(below[:, :64], da, 0.0)
                    dr = jnp.where(below, dr, 0.0)
                a[n] = a[n] - da
                rr[n] = rr[n] - dr
            fin = rr[b]
            for p in range(4):
                fin = jnp.where(sub == o + p, ur[p], fin)
            rr[b] = fin

    load_rb.wait()
    for i in range(4):
        coeff = jnp.concatenate(work_r[i], axis=0)
        hi, lo = split_hi_lo(coeff)
        basis = rbv[i]
        nb[i] = (
            lax.dot_general(hi, basis, NN, preferred_element_type=F32)
            + lax.dot_general(lo, basis, NN, preferred_element_type=F32)
        )
        p = lax.dot_general(coeff, g_ref[i], NN, precision=highest, preferred_element_type=F32)
        hi, lo = split_hi_lo(p)
        proj[i] = jnp.concatenate([hi, lo], axis=0)

    load_cp.wait()
    first = lax.broadcasted_iota(jnp.int32, (64, 128), 1) < 64
    outs = [pltpu.make_async_copy(ncv.at[pl.ds(8 * n, 8)], nc.at[pl.ds(8 * n, 8)], out_sem.at[n]) for n in range(8)]
    for n in range(8):
        for t in range(8 * n, 8 * n + 8):
            row = rows_s[t]
            coupling = cpv[t].astype(F32)
            zero = jnp.zeros_like(coupling)
            pair = jnp.concatenate(
                [jnp.where(first, coupling, zero), jnp.where(first, zero, coupling)], axis=0
            ).astype(BF16)
            both = lax.dot_general(proj[jnp.minimum(row, 3)], pair, NN, preferred_element_type=F32)
            live = jnp.where(row < 4, 1.0, 0.0)
            ncv[t] = (both[:64] + both[64:]) * live
        outs[n].start()
    for copy in outs:
        copy.wait()


def back(tile_rows, r_side, gram, rb, cp):
    any_space = pl.BlockSpec(memory_space=pl.ANY)
    vmem = pl.BlockSpec(memory_space=pltpu.VMEM)
    return pl.pallas_call(
        back_kernel,
        out_shape=(
            jax.ShapeDtypeStruct((4, 64, 128), F32),
            jax.ShapeDtypeStruct((64, 64, 128), F32),
        ),
        in_specs=[pl.BlockSpec(memory_space=pltpu.SMEM), vmem, vmem, any_space, any_space],
        out_specs=(vmem, any_space),
        scratch_shapes=[
            pltpu.VMEM((64, 64, 128), BF16),
            pltpu.VMEM((4, 128, 128), BF16),
            pltpu.VMEM((64, 64, 128), F32),
            pltpu.VMEM((4, 128, 128), BF16),
            pltpu.SemaphoreType.DMA((2,)),
            pltpu.SemaphoreType.DMA((8,)),
        ],
        compiler_params=pltpu.CompilerParams(vmem_limit_bytes=40 * 1024 * 1024),
    )(tile_rows, r_side, gram, rb, cp)


def local(row_bases, col_bases, test_matrix, couplings, tile_rows, tile_cols):
    idx = jnp.broadcast_to(jnp.concatenate([tile_cols, tile_rows])[None, :], (8, 128))
    r_side, gram = front(col_bases, test_matrix, couplings, row_bases, idx)
    return back(tile_rows, r_side, gram, row_bases, couplings)


def solution(mesh):
    in_specs = (
        P("rows", None, "cols"),
        P("cols", None, "rows"),
        P("cols", None, "rows"),
        P(("rows", "cols"), None, None),
        P(("rows", "cols")),
        P(("rows", "cols")),
    )
    out_specs = (P("rows", None, "cols"), P(("rows", "cols"), None, None))
    return jax.shard_map(local, mesh=mesh, in_specs=in_specs, out_specs=out_specs, check_vma=False)
```

time: 407 us -> 71.9 us (0.18)
  waiting for transfers between devices: 305 us -> 0 us
  Pallas kernels: 0 us -> 64.9 us
  other arithmetic: 49.2 us -> 0.75 us
  matrix products: 24.1 us -> 0 us
  between operations: 13.9 us -> 0.65 us
  local copies, waits for them, and re-layouts: 13.4 us -> 5.43 us
    all_gather x1 -> x0, waiting for transfers between devices: 154 us -> none  [local(): piece = lax.all_gather(sketch, 'cols', axis=0, tiled=True)]
    psum x2 -> x0, waiting for transfers between devices: 151 us -> none  [the longest x1 84 us: local(): row_side_sketch, gram = lax.psum((sketch_part, gram_part), 'cols')]
    pallas_call x0 -> x2, Pallas kernels: none -> 64.9 us  [the longest x1 58 us: front(): pl.pallas_call(front_kernel, out_shape=(jax.ShapeDtypeStruct((NCOL, 16, 1...]
    another operation x7 -> x0, other arithmetic: 44.1 us -> none  [the longest x4 24.3 us: local(): lower = jnp.linalg.cholesky(curvature_factor)]
    dot_general x12 -> x0, matrix products: 22.8 us -> none  [the longest x1 3.75 us: local(): jnp.einsum('jal,jkl->jak', test_matrix, col_bases, preferred_element_type...]
    gather x1 -> x0, local copies, waits for them, and re-layouts: 10.2 us -> none  [local(): picked = jnp.take(piece, jnp.clip(tile_cols, 0, count - 1), axis=0)]
  transfers between devices with their start and end apart: 3 -> 0, of which waited for: 3 -> 0; matrix products, arithmetic and copies ran while one was open for 0% -> 0% of each run, Pallas kernels for 0% -> 0%
where the time goes in v1:
time: 71.9 us; the launch traced here: 71.7 us
  Pallas kernels  64.9 us (90%)
  local copies, waits for them, and re-layouts  5.43 us (8%)
  other arithmetic  0.75 us (1%)
    pallas_call x1, Pallas kernels, front(): pl.pallas_call(front_kernel, out_shape=(jax.ShapeDtypeStruct((NCOL, 16, 1...  58 us
    pallas_call x1, Pallas kernels, back(): pl.pallas_call(back_kernel, out_shape=(jax.ShapeDtypeStruct((4, 64, 128),...  6.88 us
    unnamed x10, local copies, waits for them, and re-layouts  5.43 us

profile of v1, /device:TPU:0, one launch (start us, length us, event | category | flops | bytes accessed | tf_op | source)
XLA Modules:
  0.0 71.7 jit_solution(5870339888145350219)
XLA Ops:
  0.6 0.7 %pad_add_fusion = s32[128]{0:T(128)S(1)} fusion(s32[64]{0:T(128)} %rows_s.1, s32[64]{0:T(128)} %param.11), kind=kLoop, calls=%fused_computation | loop fusion | flops 128 | bytes 1024 | tf_op jit(solution)/shard_map/concatenate | solution.py:399
  1.4 0.0 copy-start
  1.4 1.2 %copy-done = bf16[64,64,128]{2,1,0:T(8,128)(2,1)S(1)} copy-done((bf16[64,64,128]{2,1,0:T(8,128)(2,1)S(1)}, bf16[64,64,128]{2,1,0:T(8,128)(2,1)}, u32[]{:S(2)}) %copy-start) | copy-done | bytes 1048600
  2.6 0.0 copy-start.1
  2.6 1.9 %copy-done.1 = bf16[48,128,256]{2,1,0:T(8,128)(2,1)S(1)} copy-done((bf16[48,128,256]{2,1,0:T(8,128)(2,1)S(1)}, bf16[48,128,256]{2,1,0:T(8,128)(2,1)}, u32[]{:S(2)}) %copy-start.1) | copy-done | bytes 3145752
  4.5 0.0 copy-start.2
  4.5 1.4 %copy-done.2 = bf16[48,64,256]{2,1,0:T(8,128)(2,1)S(1)} copy-done((bf16[48,64,256]{2,1,0:T(8,128)(2,1)S(1)}, bf16[48,64,256]{2,1,0:T(8,128)(2,1)}, u32[]{:S(2)}) %copy-start.2) | copy-done | bytes 1572888
  5.9 0.0 copy-start.3
  5.9 0.9 %copy-done.3 = bf16[4,128,128]{2,1,0:T(8,128)(2,1)S(1)} copy-done((bf16[4,128,128]{2,1,0:T(8,128)(2,1)S(1)}, bf16[4,128,128]{2,1,0:T(8,128)(2,1)}, u32[]{:S(2)}) %copy-start.3) | copy-done | bytes 131096
  6.8 0.0 copy-start.4
  6.8 58.0 %shard_map.77 = (f32[16,16,128]{2,1,0:T(8,128)S(1)}, f32[4,128,128]{2,1,0:T(8,128)S(1)}) custom-call(bf16[48,128,256]{2,1,0:T(8,128)(2,1)S(1)} %copy-done.1, bf16[48,64,256]{2,1,0:T(8,128)(2,1)S(1)} %copy-done.2, bf16[64,64,128]{2,1,0:T(8,128)(2,1)S(1)} %copy-done, bf16[4,128,128]{2,1,0:T(8,128)(2,1)S(1)} %copy-done.3, s32[8,128]{1,0:T(8,128)S(1)} %broadcast_in_dim.2.idx), custom_call_target="tpu_custom_call" | custom-call | tf_op jit(solution)/shard_map/pallas_call | solution.py:253
  64.8 0.0 copy-done.4
  64.8 6.9 %shard_map.78 = (f32[4,64,128]{2,1,0:T(8,128)}, f32[64,64,128]{2,1,0:T(8,128)}) custom-call(s32[64]{0:T(128)S(1)} %copy-done.4, f32[16,16,128]{2,1,0:T(8,128)S(1)} %get-tuple-element.4.r_ref, f32[4,128,128]{2,1,0:T(8,128)S(1)} %get-tuple-element.5.g_ref, bf16[4,128,128]{2,1,0:T(8,128)(2,1)S(1)} %copy-done.3, bf16[64,64,128]{2,1,0:T(8,128)(2,1)S(1)} %copy-done), custom_call_target="tpu_custom_call" | custom-call | tf_op jit(solution)/shard_map/pallas_call | solution.py:378
  (1 shorter events, 0.0 us)
Async XLA Ops:
  1.4 1.2 %copy-start = (bf16[64,64,128]{2,1,0:T(8,128)(2,1)S(1)}, bf16[64,64,128]{2,1,0:T(8,128)(2,1)}, u32[]{:S(2)}) copy-start(bf16[64,64,128]{2,1,0:T(8,128)(2,1)} %cp.3) | copy-start | bytes 3145732
  2.6 1.9 %copy-start.1 = (bf16[48,128,256]{2,1,0:T(8,128)(2,1)S(1)}, bf16[48,128,256]{2,1,0:T(8,128)(2,1)}, u32[]{:S(2)}) copy-start(bf16[48,128,256]{2,1,0:T(8,128)(2,1)} %cb.1) | copy-start | bytes 9437188
  4.5 1.4 %copy-start.2 = (bf16[48,64,256]{2,1,0:T(8,128)(2,1)S(1)}, bf16[48,64,256]{2,1,0:T(8,128)(2,1)}, u32[]{:S(2)}) copy-start(bf16[48,64,256]{2,1,0:T(8,128)(2,1)} %tm.1) | copy-start | bytes 4718596
  5.9 0.9 %copy-start.3 = (bf16[4,128,128]{2,1,0:T(8,128)(2,1)S(1)}, bf16[4,128,128]{2,1,0:T(8,128)(2,1)}, u32[]{:S(2)}) copy-start(bf16[4,128,128]{2,1,0:T(8,128)(2,1)} %rb.3) | copy-start | bytes 393220
  6.8 58.0 %copy-start.4 = (s32[64]{0:T(128)S(1)}, s32[64]{0:T(128)}, u32[]{:S(2)}) copy-start(s32[64]{0:T(128)} %rows_s.1) | copy-start | bytes 772

commit v2 on v1

--- a/solution.py
+++ b/solution.py
@@ -29,8 +29,8 @@
 
 
 def front_kernel(
-    cb, tm, cp, rb, idx, out_r, out_g,
-    cbv, tmv, rbv, part, own, prx, zr1, zr2, full, cpl, idxv, idxs,
+    cb, tm, cp, rb, tcols, trows, out_r, out_g,
+    cbv, tmv, rbv, part, own, prx, zrx, full, skb, cpl, pairs, idxv, idxs,
     gpart, grx, gall, rpart, rrx, rall,
     ld_sem, misc_sem, pc_send, pc_recv, zs_send, zs_recv, ag_send, ag_recv, fw_send, fw_recv,
     cp_send, cp_recv, ix_send, ix_recv, g1_send, g1_recv, g2_send, g2_recv,
@@ -41,43 +41,38 @@
     z, h = lax.div(r, 2), lax.rem(r, 2)
     y, x = lax.div(k, 4), lax.rem(k, 4)
     partner = (r + 1 - 2 * h, k)
-    up = (lax.rem(z + 1, 4) * 2 + h, k)
-    down = (lax.rem(z + 3, 4) * 2 + h, k)
+    along = {q: (lax.rem(z + q, 4) * 2 + h, k) for q in (1, 2, 3)}
     peers = [lax.rem(y + dy, 4) * 4 + lax.rem(x + dx, 4) for dy, dx in OFFSETS]
 
-    def zc(q):
-        return lax.rem(z + q, 4) * CH
-
-    order = (2, 1, 3, 0)
+    def piece(s, q):
+        return lax.rem(z + q, 4) * CH + s * HC
+
+    order = [(s, q) for s in (0, 1) for q in (2, 1, 3, 0)]
     loads = {}
     for n, half in enumerate((1 - h, h)):
-        for m, q in enumerate(order):
-            at = pl.ds(half * HALF + zc(q), CH)
-            a = pltpu.make_async_copy(cb.at[at], cbv.at[at], ld_sem.at[0, n * 4 + m])
-            b = pltpu.make_async_copy(tm.at[at], tmv.at[at], ld_sem.at[1, n * 4 + m])
+        for m, (s, q) in enumerate(order):
+            at = pl.ds(half * HALF + piece(s, q), HC)
+            a = pltpu.make_async_copy(cb.at[at], cbv.at[at], ld_sem.at[0, n * 8 + m])
+            b = pltpu.make_async_copy(tm.at[at], tmv.at[at], ld_sem.at[1, n * 8 + m])
             a.start()
             b.start()
-            loads[n, q] = (a, b)
+            loads[n, s, q] = (a, b)
     load_rb = pltpu.make_async_copy(rb, rbv, misc_sem.at[0])
     load_rb.start()
     own_cp = pltpu.make_async_copy(cp.at[pl.ds(4 * k, 4)], cpl.at[k], misc_sem.at[1])
     own_cp.start()
-    own_ix = pltpu.make_async_copy(idx, idxv.at[k], misc_sem.at[2])
-    own_ix.start()
 
     barrier = pltpu.get_barrier_semaphore()
-    for device in [partner, up, down] + [(r, c) for c in peers]:
+    for device in [partner, along[1], along[2], along[3]] + [(r, c) for c in peers]:
         pl.semaphore_signal(barrier, inc=1, device_id=device, device_id_type=MESH)
 
-    def sketch(n, q, dst):
-        for load in loads[n, q]:
+    def sketch(n, s, q, dst):
+        for load in loads[n, s, q]:
             load.wait()
         half = (1 - h) if n == 0 else h
-        base = half * HALF + zc(q)
-
-        @pl.loop(0, CH, unroll=True)
-        def _(u):
-            dst[zc(q) + u] = (
+        base = half * HALF + piece(s, q)
+        for u in range(HC):
+            dst[piece(s, q) + u] = (
                 lax.dot_general(tmv[base + u], cbv[base + u], NT, preferred_element_type=F32) * SCALE
             )
 
@@ -93,40 +88,31 @@
         started.append(copy)
         return copy
 
-    sketch(0, 2, part)
-    pl.semaphore_wait(barrier, 3 + len(OFFSETS))
+    for s, q in order:
+        sketch(0, s, q, part)
+    idxv[k] = jnp.broadcast_to(jnp.concatenate([tcols[...], trows[...]], axis=1), (8, 128))
+    pl.semaphore_wait(barrier, 4 + len(OFFSETS))
     to_partner = {}
-
-    def send_partner(m, q):
-        at = pl.ds(zc(q), CH)
-        to_partner[q] = go(remote(part.at[at], prx.at[at], pc_send.at[m], pc_recv.at[m], partner))
-
-    send_partner(0, 2)
+    for m, (s, q) in enumerate(order):
+        at = pl.ds(piece(s, q), HC)
+        to_partner[s, q] = go(remote(part.at[at], prx.at[at], pc_send.at[m], pc_recv.at[m], partner))
+
+    scatter = {}
+    for s, q in order:
+        sketch(1, s, q, own)
+        to_partner[s, q].wait_recv()
+        at = pl.ds(piece(s, q), HC)
+        own[at] = own[at] + prx[at]
+        if q:
+            n = 3 * s + q - 1
+            scatter[s, q] = go(remote(own.at[at], zrx.at[n], zs_send.at[n], zs_recv.at[n], along[q]))
+
     moves = []
     for n, c in enumerate(peers):
         moves.append((
             go(remote(cp.at[pl.ds(4 * c, 4)], cpl.at[k], cp_send.at[n], cp_recv.at[n], (r, c))),
-            go(remote(idx, idxv.at[k], ix_send.at[n], ix_recv.at[n], (r, c))),
+            go(remote(idxv.at[k], idxv.at[k], ix_send.at[n], ix_recv.at[n], (r, c))),
         ))
-    for m, q in enumerate(order):
-        if m:
-            sketch(0, q, part)
-            send_partner(m, q)
-
-    def add_partner(q):
-        sketch(1, q, own)
-        to_partner[q].wait_recv()
-        at = pl.ds(zc(q), CH)
-        own[at] = own[at] + prx[at]
-
-    add_partner(2)
-    a2 = go(remote(own.at[pl.ds(zc(2), HC)], zr1.at[0], zs_send.at[0], zs_recv.at[0], up))
-    b2 = go(remote(own.at[pl.ds(zc(2) + HC, HC)], zr1.at[1], zs_send.at[1], zs_recv.at[1], down))
-    add_partner(1)
-    b1 = go(remote(own.at[pl.ds(zc(1) + HC, HC)], zr2.at[1], zs_send.at[2], zs_recv.at[2], up))
-    add_partner(3)
-    a3 = go(remote(own.at[pl.ds(zc(3), HC)], zr2.at[2], zs_send.at[3], zs_recv.at[3], down))
-    add_partner(0)
 
     load_rb.wait()
     for i in range(4):
@@ -136,14 +122,26 @@
         for n, c in enumerate(peers)
     ]
 
-    a2.wait_recv()
-    at = pl.ds(zc(1), HC)
-    own[at] = own[at] + zr1[0]
-    a1 = go(remote(own.at[at], zr2.at[0], zs_send.at[4], zs_recv.at[4], up))
-    b2.wait_recv()
-    at = pl.ds(zc(3) + HC, HC)
-    own[at] = own[at] + zr1[1]
-    b3 = go(remote(own.at[at], zr2.at[3], zs_send.at[5], zs_recv.at[5], down))
+    def spread(start, send, recv, device):
+        at = pl.ds(start, HC)
+        return go(remote(full.at[at], full.at[at], send, recv, device))
+
+    def halves(start):
+        for u in range(HC):
+            hi, lo = split_hi_lo(full[start + u])
+            skb[start + u] = jnp.concatenate([hi, lo], axis=0)
+
+    gather, forwarded = {}, []
+    for s in (0, 1):
+        for q in (1, 2, 3):
+            scatter[s, q].wait_recv()
+        mine = h * HALF + piece(s, 0)
+        full[pl.ds(mine, HC)] = own[pl.ds(piece(s, 0), HC)] + zrx[3 * s] + zrx[3 * s + 1] + zrx[3 * s + 2]
+        for q in (2, 1, 3):
+            n = 3 * s + q - 1
+            gather[s, q] = spread(mine, ag_send.at[n], ag_recv.at[n], along[q])
+        forwarded.append((s, 0, spread(mine, fw_send.at[4 * s], fw_recv.at[4 * s], partner)))
+        halves(mine)
 
     for copy in gram1:
         copy.wait_recv()
@@ -156,66 +154,49 @@
         for n, c in enumerate(peers)
     ]
 
-    for copy in (b1, a3, a1, b3):
-        copy.wait_recv()
-    mine = h * HALF + zc(0)
-    at = pl.ds(zc(0), HC)
-    full[pl.ds(mine, HC)] = own[at] + zr2[0] + zr2[2]
-    at = pl.ds(zc(0) + HC, HC)
-    full[pl.ds(mine + HC, HC)] = own[at] + zr2[1] + zr2[3]
-
-    def spread(start, count, send, recv, device):
-        at = pl.ds(start, count)
-        return go(remote(full.at[at], full.at[at], send, recv, device))
-
-    g_up = spread(mine, CH, ag_send.at[0], ag_recv.at[0], up)
-    g_down = spread(mine, CH, ag_send.at[1], ag_recv.at[1], down)
-    forwarded = [spread(mine, CH, fw_send.at[0], fw_recv.at[0], partner)]
-    g_up.wait_recv()
-    below = h * HALF + zc(3)
-    f_up = spread(below, HC, ag_send.at[2], ag_recv.at[2], up)
-    forwarded.append(spread(below, CH, fw_send.at[1], fw_recv.at[1], partner))
-    g_down.wait_recv()
-    above = h * HALF + zc(1)
-    f_down = spread(above + HC, HC, ag_send.at[3], ag_recv.at[3], down)
-    forwarded.append(spread(above, CH, fw_send.at[2], fw_recv.at[2], partner))
-    far = h * HALF + zc(2)
-    f_up.wait_recv()
-    forwarded.append(spread(far, HC, fw_send.at[3], fw_recv.at[3], partner))
-    f_down.wait_recv()
-    forwarded.append(spread(far + HC, HC, fw_send.at[4], fw_recv.at[4], partner))
+    for s in (0, 1):
+        for q in (1, 3, 2):
+            gather[s, q].wait_recv()
+            n = 4 * s + q
+            start = h * HALF + piece(s, 4 - q)
+            forwarded.append((s, 4 - q, spread(start, fw_send.at[n], fw_recv.at[n], partner)))
+            halves(start)
 
     own_cp.wait()
-    own_ix.wait()
     for a, b in moves:
         a.wait_recv()
         b.wait_recv()
-    to_scalars = pltpu.make_async_copy(idxv, idxs, misc_sem.at[3])
+    to_scalars = pltpu.make_async_copy(idxv, idxs, misc_sem.at[2])
     to_scalars.start()
+    first = lax.broadcasted_iota(jnp.int32, (64, 128), 1) < 64
+
+    @pl.loop(0, NCOL)
+    def _(c):
+        for s in range(4):
+            coupling = cpl[c, s].astype(F32)
+            zero = jnp.zeros_like(coupling)
+            pairs[4 * c + s] = jnp.concatenate(
+                [jnp.where(first, coupling, zero), jnp.where(first, zero, coupling)], axis=0
+            ).astype(BF16)
+
     to_scalars.wait()
-    for copy in forwarded:
-        copy.wait_recv()
-
-    first = lax.broadcasted_iota(jnp.int32, (64, 128), 1) < 64
-
-    def tiles(c, carry):
+    for s, q, copy in forwarded:
+        copy.wait_recv()
+        halves((1 - h) * HALF + piece(s, q))
+
+    def tiles(n, carry):
         sums = list(carry)
-        for s in range(4):
+        for m in range(8):
+            c, s = 2 * n + m // 4, m % 4
             j = jnp.clip(idxs[c, 0, 4 * k + s] - CB * k, 0, CB - 1)
             row = idxs[c, 0, 64 + 4 * k + s]
-            hi, lo = split_hi_lo(full[j])
-            coupling = cpl[c, s].astype(F32)
-            zero = jnp.zeros_like(coupling)
-            pair = jnp.concatenate(
-                [jnp.where(first, coupling, zero), jnp.where(first, zero, coupling)], axis=0
-            ).astype(BF16)
-            both = lax.dot_general(jnp.concatenate([hi, lo], axis=0), pair, NT, preferred_element_type=F32)
+            both = lax.dot_general(skb[j], pairs[4 * c + s], NT, preferred_element_type=F32)
             term = both[:64] + both[64:]
             for i in range(4):
                 sums[i] = sums[i] + jnp.where(row == i, 1.0, 0.0) * term
         return tuple(sums)
 
-    sums = lax.fori_loop(0, NCOL, tiles, (jnp.zeros((64, 128), F32),) * 4)
+    sums = lax.fori_loop(0, NCOL // 2, tiles, (jnp.zeros((64, 128), F32),) * 4)
     for i in range(4):
         rpart[pl.ds(4 * i, 4)] = sums[i].reshape(4, 16, 128)
 
@@ -223,6 +204,11 @@
         go(remote(rpart.at[c], rrx.at[n], r1_send.at[n], r1_recv.at[n], (r, c)))
         for n, c in enumerate(peers)
     ]
+    for copy in gram2:
+        copy.wait_recv()
+    for c in range(NCOL):
+        for i in range(4):
+            out_g[i, pl.ds(8 * c, 8)] = gall[c, :, pl.ds(128 * i, 128)]
     for copy in row1:
         copy.wait_recv()
     total = rpart[k]
@@ -233,11 +219,6 @@
         go(remote(rall.at[k], rall.at[k], r2_send.at[n], r2_recv.at[n], (r, c)))
         for n, c in enumerate(peers)
     ]
-    for copy in gram2:
-        copy.wait_recv()
-    for c in range(NCOL):
-        for i in range(4):
-            out_g[i, pl.ds(8 * c, 8)] = gall[c, :, pl.ds(128 * i, 128)]
     for copy in row2:
         copy.wait_recv()
     out_r[...] = rall[...]
@@ -245,7 +226,7 @@
         copy.wait_send()
 
 
-def front(cb, tm, cp, rb, idx):
+def front(cb, tm, cp, rb, tcols, trows):
     any_space = pl.BlockSpec(memory_space=pl.ANY)
     vmem = pl.BlockSpec(memory_space=pltpu.VMEM)
     dma = pltpu.SemaphoreType.DMA
@@ -256,7 +237,7 @@
             jax.ShapeDtypeStruct((NCOL, 16, 128), F32),
             jax.ShapeDtypeStruct((4, 128, 128), F32),
         ),
-        in_specs=[any_space] * 5,
+        in_specs=[any_space] * 4 + [vmem] * 2,
         out_specs=(vmem, vmem),
         scratch_shapes=[
             pltpu.VMEM((CB, 128, 256), BF16),
@@ -265,10 +246,11 @@
             pltpu.VMEM((HALF, 64, 128), F32),
             pltpu.VMEM((HALF, 64, 128), F32),
             pltpu.VMEM((HALF, 64, 128), F32),
-            pltpu.VMEM((2, HC, 64, 128), F32),
-            pltpu.VMEM((4, HC, 64, 128), F32),
+            pltpu.VMEM((6, HC, 64, 128), F32),
             pltpu.VMEM((CB, 64, 128), F32),
+            pltpu.VMEM((CB, 128, 128), BF16),
             pltpu.VMEM((NCOL, 4, 64, 128), BF16),
+            pltpu.VMEM((64, 128, 128), BF16),
             pltpu.VMEM((NCOL, 8, 128), jnp.int32),
             pltpu.SMEM((NCOL, 8, 128), jnp.int32),
             pltpu.VMEM((128, 512), F32),
@@ -277,13 +259,13 @@
             pltpu.VMEM((NCOL, 16, 128), F32),
             pltpu.VMEM((peers, 16, 128), F32),
             pltpu.VMEM((NCOL, 16, 128), F32),
-            dma((2, 8)), dma((4,)),
-            dma((4,)), dma((4,)), dma((6,)), dma((6,)), dma((4,)), dma((4,)), dma((5,)), dma((5,)),
+            dma((2, 16)), dma((3,)),
+            dma((8,)), dma((8,)), dma((6,)), dma((6,)), dma((6,)), dma((6,)), dma((8,)), dma((8,)),
         ] + [dma((peers,))] * 12,
         compiler_params=pltpu.CompilerParams(
-            collective_id=0, has_side_effects=True, vmem_limit_bytes=40 * 1024 * 1024
+            collective_id=0, has_side_effects=True, vmem_limit_bytes=60 * 1024 * 1024
         ),
-    )(cb, tm, cp, rb, idx)
+    )(cb, tm, cp, rb, tcols, trows)
 
 
 def back_kernel(rows_s, r_ref, g_ref, rb, cp, nb, nc, cpv, rbv, ncv, proj, sem, out_sem):
@@ -391,13 +373,14 @@
             pltpu.SemaphoreType.DMA((2,)),
             pltpu.SemaphoreType.DMA((8,)),
         ],
-        compiler_params=pltpu.CompilerParams(vmem_limit_bytes=40 * 1024 * 1024),
+        compiler_params=pltpu.CompilerParams(vmem_limit_bytes=60 * 1024 * 1024),
     )(tile_rows, r_side, gram, rb, cp)
 
 
 def local(row_bases, col_bases, test_matrix, couplings, tile_rows, tile_cols):
-    idx = jnp.broadcast_to(jnp.concatenate([tile_cols, tile_rows])[None, :], (8, 128))
-    r_side, gram = front(col_bases, test_matrix, couplings, row_bases, idx)
+    r_side, gram = front(
+        col_bases, test_matrix, couplings, row_bases, tile_cols.reshape(1, 64), tile_rows.reshape(1, 64)
+    )
     return back(tile_rows, r_side, gram, row_bases, couplings)
 
 

time: 71.9 us -> 56.5 us (0.79)
  Pallas kernels: 64.9 us -> 55.7 us
  local copies, waits for them, and re-layouts: 5.43 us -> 0 us
  other arithmetic: 0.75 us -> 0 us
    pallas_call x1, Pallas kernels: 58 us -> 48.6 us  [front(): pl.pallas_call(front_kernel, out_shape=(jax.ShapeDtypeStruct((NCOL, 16, 1...]
    unnamed x10 -> x0, local copies, waits for them, and re-layouts: 5.43 us -> none
    concatenate x1 -> x0, other arithmetic: 0.75 us -> none  [local(): jnp.concatenate([tile_cols, tile_rows])[None, :]]
where the time goes in v2:
time: 56.5 us; the launch traced here: 56.3 us
  Pallas kernels  55.7 us (99%)
  between operations  0.64 us (1%)
    pallas_call x1, Pallas kernels, front(): pl.pallas_call(front_kernel, out_shape=(jax.ShapeDtypeStruct((NCOL, 16, 1...  48.6 us
    pallas_call x1, Pallas kernels, back(): pl.pallas_call(back_kernel, out_shape=(jax.ShapeDtypeStruct((4, 64, 128),...  7.12 us

profile of v2, /device:TPU:0, one launch (start us, length us, event | category | flops | bytes accessed | tf_op | source)
XLA Modules:
  0.0 56.3 jit_solution(6338300960608382082)
XLA Ops:
  0.6 48.6 %shard_map.77 = (f32[16,16,128]{2,1,0:T(8,128)}, f32[4,128,128]{2,1,0:T(8,128)}) custom-call(bf16[48,128,256]{2,1,0:T(8,128)(2,1)} %cb.1, bf16[48,64,256]{2,1,0:T(8,128)(2,1)} %tm.1, bf16[64,64,128]{2,1,0:T(8,128)(2,1)} %cp.3, bf16[4,128,128]{2,1,0:T(8,128)(2,1)} %rb.3, s32[1,64]{1,0:T(1,128)} %bitcast.3, s32[1,64]{1,0:T(1,128)} %bitcast.2), custom_call_target="tpu_custom_call" | custom-call | tf_op jit(solution)/shard_map/pallas_call | solution.py:234
  49.2 7.1 %shard_map.78 = (f32[4,64,128]{2,1,0:T(8,128)}, f32[64,64,128]{2,1,0:T(8,128)}) custom-call(s32[64]{0:T(128)} %rows_s.1, f32[16,16,128]{2,1,0:T(8,128)} %get-tuple-element.4.r_ref, f32[4,128,128]{2,1,0:T(8,128)} %get-tuple-element.5.g_ref, bf16[4,128,128]{2,1,0:T(8,128)(2,1)} %rb.3, bf16[64,64,128]{2,1,0:T(8,128)(2,1)} %cp.3), custom_call_target="tpu_custom_call" | custom-call | tf_op jit(solution)/shard_map/pallas_call | solution.py:360

commit v3 on v2

--- a/solution.py
+++ b/solution.py
@@ -20,7 +20,13 @@
 NCOL = 16
 NT = (((1,), (1,)), ((), ()))
 NN = (((1,), (0,)), ((), ()))
-OFFSETS = [(dy, dx) for dy in range(4) for dx in range(4) if (dy, dx) != (0, 0)]
+OFFSETS = sorted(
+    [(dy, dx) for dy in range(4) for dx in range(4) if (dy, dx) != (0, 0)],
+    key=lambda o: -min(o[0], 4 - o[0]) - min(o[1], 4 - o[1]),
+)
+
+
+STEPS = 32400.0
 
 
 def split_hi_lo(value):
@@ -28,9 +34,24 @@
     return hi, (value - hi.astype(F32)).astype(BF16)
 
 
+def code(value):
+    head = value.astype(BF16)
+    base = head.astype(F32)
+    rest = (value - base) * pl.reciprocal(jnp.maximum(jnp.abs(base), 1e-30), approx=True)
+    steps = jnp.floor(rest * STEPS + 0.5)
+    return head, (steps[:32] * 256.0 + steps[32:]).astype(jnp.int32).astype(jnp.int16)
+
+
+def rest_of(head, word):
+    word = word.astype(jnp.int32)
+    top = (word + 128) >> 8
+    steps = jnp.concatenate([top, word - top * 256], axis=0).astype(F32)
+    return jnp.abs(head.astype(F32)) * (steps * (1.0 / STEPS))
+
+
 def front_kernel(
     cb, tm, cp, rb, tcols, trows, out_r, out_g,
-    cbv, tmv, rbv, part, own, prx, zrx, full, skb, cpl, pairs, idxv, idxs,
+    cbv, tmv, rbv, part, own, prx, zsh, zsw, zrh, zrw, skw, skb, cpl, pairs, idxv, idxs,
     gpart, grx, gall, rpart, rrx, rall,
     ld_sem, misc_sem, pc_send, pc_recv, zs_send, zs_recv, ag_send, ag_recv, fw_send, fw_recv,
     cp_send, cp_recv, ix_send, ix_recv, g1_send, g1_recv, g2_send, g2_recv,
@@ -90,29 +111,37 @@
 
     for s, q in order:
         sketch(0, s, q, part)
-    idxv[k] = jnp.broadcast_to(jnp.concatenate([tcols[...], trows[...]], axis=1), (8, 128))
+    idxv[k] = jnp.concatenate([tcols[...], trows[...]], axis=1)
     pl.semaphore_wait(barrier, 4 + len(OFFSETS))
     to_partner = {}
     for m, (s, q) in enumerate(order):
         at = pl.ds(piece(s, q), HC)
         to_partner[s, q] = go(remote(part.at[at], prx.at[at], pc_send.at[m], pc_recv.at[m], partner))
+    labels = [
+        go(remote(idxv.at[k], idxv.at[k], ix_send.at[n], ix_recv.at[n], (r, c)))
+        for n, c in enumerate(peers)
+    ]
+    moves = [
+        go(remote(cp.at[pl.ds(4 * c, 4)], cpl.at[k], cp_send.at[n], cp_recv.at[n], (r, c)))
+        for n, c in enumerate(peers)
+    ]
 
     scatter = {}
     for s, q in order:
         sketch(1, s, q, own)
         to_partner[s, q].wait_recv()
-        at = pl.ds(piece(s, q), HC)
-        own[at] = own[at] + prx[at]
-        if q:
-            n = 3 * s + q - 1
-            scatter[s, q] = go(remote(own.at[at], zrx.at[n], zs_send.at[n], zs_recv.at[n], along[q]))
-
-    moves = []
-    for n, c in enumerate(peers):
-        moves.append((
-            go(remote(cp.at[pl.ds(4 * c, 4)], cpl.at[k], cp_send.at[n], cp_recv.at[n], (r, c))),
-            go(remote(idxv.at[k], idxv.at[k], ix_send.at[n], ix_recv.at[n], (r, c))),
-        ))
+        at = piece(s, q)
+        if not q:
+            own[pl.ds(at, HC)] = own[pl.ds(at, HC)] + prx[pl.ds(at, HC)]
+            continue
+        n = 3 * s + q - 1
+        for u in range(HC):
+            zsh[n, u], zsw[n, u] = code(own[at + u] + prx[at + u])
+        scatter[s, q] = (
+            go(remote(zsh.at[n], zrh.at[n], zs_send.at[2 * n], zs_recv.at[2 * n], along[q])),
+            go(remote(zsw.at[n], zrw.at[n], zs_send.at[2 * n + 1], zs_recv.at[2 * n + 1], along[q])),
+        )
+
 
     load_rb.wait()
     for i in range(4):
@@ -122,50 +151,50 @@
         for n, c in enumerate(peers)
     ]
 
-    def spread(start, send, recv, device):
-        at = pl.ds(start, HC)
-        return go(remote(full.at[at], full.at[at], send, recv, device))
-
-    def halves(start):
+    def spread(start, send, recv, n, device):
+        heads = skb.at[pl.ds(start, HC), pl.ds(0, 64)]
+        words = skw.at[pl.ds(start, HC)]
+        return (
+            go(remote(heads, heads, send.at[2 * n], recv.at[2 * n], device)),
+            go(remote(words, words, send.at[2 * n + 1], recv.at[2 * n + 1], device)),
+        )
+
+    def arrived(copies):
+        for copy in copies:
+            copy.wait_recv()
+
+    def rests(start):
         for u in range(HC):
-            hi, lo = split_hi_lo(full[start + u])
-            skb[start + u] = jnp.concatenate([hi, lo], axis=0)
+            skb[start + u, 64:] = rest_of(skb[start + u, :64], skw[start + u]).astype(BF16)
 
     gather, forwarded = {}, []
     for s in (0, 1):
         for q in (1, 2, 3):
-            scatter[s, q].wait_recv()
+            arrived(scatter[s, q])
         mine = h * HALF + piece(s, 0)
-        full[pl.ds(mine, HC)] = own[pl.ds(piece(s, 0), HC)] + zrx[3 * s] + zrx[3 * s + 1] + zrx[3 * s + 2]
+        for u in range(HC):
+            total = own[piece(s, 0) + u]
+            for n in range(3 * s, 3 * s + 3):
+                head = zrh[n, u]
+                total = total + (head.astype(F32) + rest_of(head, zrw[n, u]))
+            skb[mine + u, :64], skw[mine + u] = code(total)
         for q in (2, 1, 3):
-            n = 3 * s + q - 1
-            gather[s, q] = spread(mine, ag_send.at[n], ag_recv.at[n], along[q])
-        forwarded.append((s, 0, spread(mine, fw_send.at[4 * s], fw_recv.at[4 * s], partner)))
-        halves(mine)
-
-    for copy in gram1:
-        copy.wait_recv()
-    total = gpart[pl.ds(pl.multiple_of(8 * k, 8), 8)]
-    for n in range(len(OFFSETS)):
-        total = total + grx[n]
-    gall[k] = total
-    gram2 = [
-        go(remote(gall.at[k], gall.at[k], g2_send.at[n], g2_recv.at[n], (r, c)))
-        for n, c in enumerate(peers)
-    ]
+            gather[s, q] = spread(mine, ag_send, ag_recv, 3 * s + q - 1, along[q])
+        forwarded.append((s, 0, spread(mine, fw_send, fw_recv, 4 * s, partner)))
+        rests(mine)
 
     for s in (0, 1):
         for q in (1, 3, 2):
-            gather[s, q].wait_recv()
-            n = 4 * s + q
+            arrived(gather[s, q])
             start = h * HALF + piece(s, 4 - q)
-            forwarded.append((s, 4 - q, spread(start, fw_send.at[n], fw_recv.at[n], partner)))
-            halves(start)
+            forwarded.append((s, 4 - q, spread(start, fw_send, fw_recv, 4 * s + q, partner)))
+            rests(start)
 
     own_cp.wait()
-    for a, b in moves:
-        a.wait_recv()
-        b.wait_recv()
+    for copy in labels:
+        copy.wait_recv()
+    for copy in moves:
+        copy.wait_recv()
     to_scalars = pltpu.make_async_copy(idxv, idxs, misc_sem.at[2])
     to_scalars.start()
     first = lax.broadcasted_iota(jnp.int32, (64, 128), 1) < 64
@@ -180,9 +209,19 @@
             ).astype(BF16)
 
     to_scalars.wait()
-    for s, q, copy in forwarded:
-        copy.wait_recv()
-        halves((1 - h) * HALF + piece(s, q))
+    for s, q, copies in forwarded:
+        arrived(copies)
+        rests((1 - h) * HALF + piece(s, q))
+    for copy in gram1:
+        copy.wait_recv()
+    total = gpart[pl.ds(pl.multiple_of(8 * k, 8), 8)]
+    for n in range(len(OFFSETS)):
+        total = total + grx[n]
+    gall[k] = total
+    gram2 = [
+        go(remote(gall.at[k], gall.at[k], g2_send.at[n], g2_recv.at[n], (r, c)))
+        for n, c in enumerate(peers)
+    ]
 
     def tiles(n, carry):
         sums = list(carry)
@@ -246,13 +285,16 @@
             pltpu.VMEM((HALF, 64, 128), F32),
             pltpu.VMEM((HALF, 64, 128), F32),
             pltpu.VMEM((HALF, 64, 128), F32),
-            pltpu.VMEM((6, HC, 64, 128), F32),
-            pltpu.VMEM((CB, 64, 128), F32),
+            pltpu.VMEM((6, HC, 64, 128), BF16),
+            pltpu.VMEM((6, HC, 32, 128), jnp.int16),
+            pltpu.VMEM((6, HC, 64, 128), BF16),
+            pltpu.VMEM((6, HC, 32, 128), jnp.int16),
+            pltpu.VMEM((CB, 32, 128), jnp.int16),
             pltpu.VMEM((CB, 128, 128), BF16),
             pltpu.VMEM((NCOL, 4, 64, 128), BF16),
             pltpu.VMEM((64, 128, 128), BF16),
-            pltpu.VMEM((NCOL, 8, 128), jnp.int32),
-            pltpu.SMEM((NCOL, 8, 128), jnp.int32),
+            pltpu.VMEM((NCOL, 1, 128), jnp.int32),
+            pltpu.SMEM((NCOL, 1, 128), jnp.int32),
             pltpu.VMEM((128, 512), F32),
             pltpu.VMEM((peers, 8, 512), F32),
             pltpu.VMEM((NCOL, 8, 512), F32),
@@ -260,7 +302,7 @@
             pltpu.VMEM((peers, 16, 128), F32),
             pltpu.VMEM((NCOL, 16, 128), F32),
             dma((2, 16)), dma((3,)),
-            dma((8,)), dma((8,)), dma((6,)), dma((6,)), dma((6,)), dma((6,)), dma((8,)), dma((8,)),
+            dma((8,)), dma((8,)), dma((12,)), dma((12,)), dma((12,)), dma((12,)), dma((16,)), dma((16,)),
         ] + [dma((peers,))] * 12,
         compiler_params=pltpu.CompilerParams(
             collective_id=0, has_side_effects=True, vmem_limit_bytes=60 * 1024 * 1024

time: 56.5 us -> 50.6 us (0.90)
  Pallas kernels: 55.7 us -> 49.7 us
    pallas_call x1, Pallas kernels: 48.6 us -> 42.6 us  [front(): pl.pallas_call(front_kernel, out_shape=(jax.ShapeDtypeStruct((NCOL, 16, 1...]
where the time goes in v3:
time: 50.6 us; the launch traced here: 50.4 us
  Pallas kernels  49.7 us (98%)
  between operations  0.64 us (1%)
    pallas_call x1, Pallas kernels, front(): pl.pallas_call(front_kernel, out_shape=(jax.ShapeDtypeStruct((NCOL, 16, 1...  42.6 us
    pallas_call x1, Pallas kernels, back(): pl.pallas_call(back_kernel, out_shape=(jax.ShapeDtypeStruct((4, 64, 128),...  7.12 us

profile of v3, /device:TPU:0, one launch (start us, length us, event | category | flops | bytes accessed | tf_op | source)
XLA Modules:
  0.0 50.4 jit_solution(14283636514537834341)
XLA Ops:
  0.6 42.6 %shard_map.77 = (f32[16,16,128]{2,1,0:T(8,128)}, f32[4,128,128]{2,1,0:T(8,128)}) custom-call(bf16[48,128,256]{2,1,0:T(8,128)(2,1)} %cb.1, bf16[48,64,256]{2,1,0:T(8,128)(2,1)} %tm.1, bf16[64,64,128]{2,1,0:T(8,128)(2,1)} %cp.3, bf16[4,128,128]{2,1,0:T(8,128)(2,1)} %rb.3, s32[1,64]{1,0:T(1,128)} %bitcast.3, s32[1,64]{1,0:T(1,128)} %bitcast.2), custom_call_target="tpu_custom_call" | custom-call | tf_op jit(solution)/shard_map/pallas_call | solution.py:273
  43.2 7.1 %shard_map.78 = (f32[4,64,128]{2,1,0:T(8,128)}, f32[64,64,128]{2,1,0:T(8,128)}) custom-call(s32[64]{0:T(128)} %rows_s.1, f32[16,16,128]{2,1,0:T(8,128)} %get-tuple-element.4.r_ref, f32[4,128,128]{2,1,0:T(8,128)} %get-tuple-element.5.g_ref, bf16[4,128,128]{2,1,0:T(8,128)(2,1)} %rb.3, bf16[64,64,128]{2,1,0:T(8,128)(2,1)} %cp.3), custom_call_target="tpu_custom_call" | custom-call | tf_op jit(solution)/shard_map/pallas_call | solution.py:402

commit v4 on v3

--- a/solution.py
+++ b/solution.py
@@ -16,8 +16,10 @@
 CB = 48
 HALF = 24
 CH = 6
-HC = 3
+SUBS = 2
+HC = CH // SUBS
 NCOL = 16
+STEP = 64
 NT = (((1,), (1,)), ((), ()))
 NN = (((1,), (0,)), ((), ()))
 OFFSETS = sorted(
@@ -68,13 +70,13 @@
     def piece(s, q):
         return lax.rem(z + q, 4) * CH + s * HC
 
-    order = [(s, q) for s in (0, 1) for q in (2, 1, 3, 0)]
+    order = [(s, q) for s in range(SUBS) for q in (2, 1, 3, 0)]
     loads = {}
     for n, half in enumerate((1 - h, h)):
         for m, (s, q) in enumerate(order):
             at = pl.ds(half * HALF + piece(s, q), HC)
-            a = pltpu.make_async_copy(cb.at[at], cbv.at[at], ld_sem.at[0, n * 8 + m])
-            b = pltpu.make_async_copy(tm.at[at], tmv.at[at], ld_sem.at[1, n * 8 + m])
+            a = pltpu.make_async_copy(cb.at[at], cbv.at[at], ld_sem.at[0, 4 * SUBS * n + m])
+            b = pltpu.make_async_copy(tm.at[at], tmv.at[at], ld_sem.at[1, 4 * SUBS * n + m])
             a.start()
             b.start()
             loads[n, s, q] = (a, b)
@@ -112,6 +114,9 @@
     for s, q in order:
         sketch(0, s, q, part)
     idxv[k] = jnp.concatenate([tcols[...], trows[...]], axis=1)
+    load_rb.wait()
+    for i in range(4):
+        gpart[:, pl.ds(i * 128, 128)] = lax.dot_general(rbv[i], rbv[i], NT, preferred_element_type=F32) * (1.0 / LEAF)
     pl.semaphore_wait(barrier, 4 + len(OFFSETS))
     to_partner = {}
     for m, (s, q) in enumerate(order):
@@ -119,6 +124,10 @@
         to_partner[s, q] = go(remote(part.at[at], prx.at[at], pc_send.at[m], pc_recv.at[m], partner))
     labels = [
         go(remote(idxv.at[k], idxv.at[k], ix_send.at[n], ix_recv.at[n], (r, c)))
+        for n, c in enumerate(peers)
+    ]
+    gram1 = [
+        go(remote(gpart.at[pl.ds(8 * c, 8)], grx.at[n], g1_send.at[n], g1_recv.at[n], (r, c)))
         for n, c in enumerate(peers)
     ]
     moves = [
@@ -143,14 +152,6 @@
         )
 
 
-    load_rb.wait()
-    for i in range(4):
-        gpart[:, pl.ds(i * 128, 128)] = lax.dot_general(rbv[i], rbv[i], NT, preferred_element_type=F32) * (1.0 / LEAF)
-    gram1 = [
-        go(remote(gpart.at[pl.ds(8 * c, 8)], grx.at[n], g1_send.at[n], g1_recv.at[n], (r, c)))
-        for n, c in enumerate(peers)
-    ]
-
     def spread(start, send, recv, n, device):
         heads = skb.at[pl.ds(start, HC), pl.ds(0, 64)]
         words = skw.at[pl.ds(start, HC)]
@@ -168,7 +169,7 @@
             skb[start + u, 64:] = rest_of(skb[start + u, :64], skw[start + u]).astype(BF16)
 
     gather, forwarded = {}, []
-    for s in (0, 1):
+    for s in range(SUBS):
         for q in (1, 2, 3):
             arrived(scatter[s, q])
         mine = h * HALF + piece(s, 0)
@@ -182,8 +183,18 @@
             gather[s, q] = spread(mine, ag_send, ag_recv, 3 * s + q - 1, along[q])
         forwarded.append((s, 0, spread(mine, fw_send, fw_recv, 4 * s, partner)))
         rests(mine)
-
-    for s in (0, 1):
+    for copy in gram1:
+        copy.wait_recv()
+    total = gpart[pl.ds(pl.multiple_of(8 * k, 8), 8)]
+    for n in range(len(OFFSETS)):
+        total = total + grx[n]
+    gall[k] = total
+    gram2 = [
+        go(remote(gall.at[k], gall.at[k], g2_send.at[n], g2_recv.at[n], (r, c)))
+        for n, c in enumerate(peers)
+    ]
+
+    for s in range(SUBS):
         for q in (1, 3, 2):
             arrived(gather[s, q])
             start = h * HALF + piece(s, 4 - q)
@@ -212,21 +223,11 @@
     for s, q, copies in forwarded:
         arrived(copies)
         rests((1 - h) * HALF + piece(s, q))
-    for copy in gram1:
-        copy.wait_recv()
-    total = gpart[pl.ds(pl.multiple_of(8 * k, 8), 8)]
-    for n in range(len(OFFSETS)):
-        total = total + grx[n]
-    gall[k] = total
-    gram2 = [
-        go(remote(gall.at[k], gall.at[k], g2_send.at[n], g2_recv.at[n], (r, c)))
-        for n, c in enumerate(peers)
-    ]
 
     def tiles(n, carry):
         sums = list(carry)
-        for m in range(8):
-            c, s = 2 * n + m // 4, m % 4
+        for m in range(STEP):
+            c, s = STEP // 4 * n + m // 4, m % 4
             j = jnp.clip(idxs[c, 0, 4 * k + s] - CB * k, 0, CB - 1)
             row = idxs[c, 0, 64 + 4 * k + s]
             both = lax.dot_general(skb[j], pairs[4 * c + s], NT, preferred_element_type=F32)
@@ -235,7 +236,7 @@
                 sums[i] = sums[i] + jnp.where(row == i, 1.0, 0.0) * term
         return tuple(sums)
 
-    sums = lax.fori_loop(0, NCOL // 2, tiles, (jnp.zeros((64, 128), F32),) * 4)
+    sums = lax.fori_loop(0, 64 // STEP, tiles, (jnp.zeros((64, 128), F32),) * 4)
     for i in range(4):
         rpart[pl.ds(4 * i, 4)] = sums[i].reshape(4, 16, 128)
 
@@ -273,8 +274,8 @@
     return pl.pallas_call(
         front_kernel,
         out_shape=(
-            jax.ShapeDtypeStruct((NCOL, 16, 128), F32),
-            jax.ShapeDtypeStruct((4, 128, 128), F32),
+            pltpu.VMEM((NCOL, 16, 128), F32),
+            pltpu.VMEM((4, 128, 128), F32),
         ),
         in_specs=[any_space] * 4 + [vmem] * 2,
         out_specs=(vmem, vmem),
@@ -285,10 +286,10 @@
             pltpu.VMEM((HALF, 64, 128), F32),
             pltpu.VMEM((HALF, 64, 128), F32),
             pltpu.VMEM((HALF, 64, 128), F32),
-            pltpu.VMEM((6, HC, 64, 128), BF16),
-            pltpu.VMEM((6, HC, 32, 128), jnp.int16),
-            pltpu.VMEM((6, HC, 64, 128), BF16),
-            pltpu.VMEM((6, HC, 32, 128), jnp.int16),
+            pltpu.VMEM((3 * SUBS, HC, 64, 128), BF16),
+            pltpu.VMEM((3 * SUBS, HC, 32, 128), jnp.int16),
+            pltpu.VMEM((3 * SUBS, HC, 64, 128), BF16),
+            pltpu.VMEM((3 * SUBS, HC, 32, 128), jnp.int16),
             pltpu.VMEM((CB, 32, 128), jnp.int16),
             pltpu.VMEM((CB, 128, 128), BF16),
             pltpu.VMEM((NCOL, 4, 64, 128), BF16),
@@ -301,9 +302,9 @@
             pltpu.VMEM((NCOL, 16, 128), F32),
             pltpu.VMEM((peers, 16, 128), F32),
             pltpu.VMEM((NCOL, 16, 128), F32),
-            dma((2, 16)), dma((3,)),
-            dma((8,)), dma((8,)), dma((12,)), dma((12,)), dma((12,)), dma((12,)), dma((16,)), dma((16,)),
-        ] + [dma((peers,))] * 12,
+            dma((2, 8 * SUBS)), dma((3,)),
+            dma((4 * SUBS,)), dma((4 * SUBS,)),
+        ] + [dma((6 * SUBS,))] * 4 + [dma((8 * SUBS,))] * 2 + [dma((peers,))] * 12,
         compiler_params=pltpu.CompilerParams(
             collective_id=0, has_side_effects=True, vmem_limit_bytes=60 * 1024 * 1024
         ),
@@ -423,6 +424,8 @@
     r_side, gram = front(
         col_bases, test_matrix, couplings, row_bases, tile_cols.reshape(1, 64), tile_rows.reshape(1, 64)
     )
+    r_side = pltpu.with_memory_space_constraint(r_side, pltpu.VMEM)
+    gram = pltpu.with_memory_space_constraint(gram, pltpu.VMEM)
     return back(tile_rows, r_side, gram, row_bases, couplings)
 
 

time: 50.6 us -> 48.3 us (0.955)
  Pallas kernels: 49.7 us -> 47.6 us
    pallas_call x1, Pallas kernels: 42.6 us -> 40.8 us  [front(): pl.pallas_call(front_kernel, out_shape=(pltpu.VMEM((NCOL, 16, 128), F32),...]
where the time goes in v4:
time: 48.3 us; the launch traced here: 48.2 us
  Pallas kernels  47.6 us (99%)
  between operations  0.64 us (1%)
    pallas_call x1, Pallas kernels, front(): pl.pallas_call(front_kernel, out_shape=(pltpu.VMEM((NCOL, 16, 128), F32),...  40.8 us
    pallas_call x1, Pallas kernels, back(): pl.pallas_call(back_kernel, out_shape=(jax.ShapeDtypeStruct((4, 64, 128),...  6.76 us

profile of v4, /device:TPU:0, one launch (start us, length us, event | category | flops | bytes accessed | tf_op | source)
XLA Modules:
  0.0 48.2 jit_solution(7191403549151944988)
XLA Ops:
  0.6 40.8 %shard_map.77 = (f32[16,16,128]{2,1,0:T(8,128)S(1)}, f32[4,128,128]{2,1,0:T(8,128)S(1)}) custom-call(bf16[48,128,256]{2,1,0:T(8,128)(2,1)} %cb.1, bf16[48,64,256]{2,1,0:T(8,128)(2,1)} %tm.1, bf16[64,64,128]{2,1,0:T(8,128)(2,1)} %cp.3, bf16[4,128,128]{2,1,0:T(8,128)(2,1)} %rb.3, s32[1,64]{1,0:T(1,128)} %bitcast.3, s32[1,64]{1,0:T(1,128)} %bitcast.2), custom_call_target="tpu_custom_call" | custom-call | tf_op jit(solution)/shard_map/pallas_call | solution.py:274
  41.4 6.8 %shard_map.78 = (f32[4,64,128]{2,1,0:T(8,128)}, f32[64,64,128]{2,1,0:T(8,128)}) custom-call(s32[64]{0:T(128)} %rows_s.1, f32[16,16,128]{2,1,0:T(8,128)S(1)} %get-tuple-element.4.r_ref, f32[4,128,128]{2,1,0:T(8,128)S(1)} %get-tuple-element.5.g_ref, bf16[4,128,128]{2,1,0:T(8,128)(2,1)} %rb.3, bf16[64,64,128]{2,1,0:T(8,128)(2,1)} %cp.3), custom_call_target="tpu_custom_call" | custom-call | tf_op jit(solution)/shard_map/pallas_call | solution.py:403

commit v5 on v4

--- a/solution.py
+++ b/solution.py
@@ -20,6 +20,7 @@
 HC = CH // SUBS
 NCOL = 16
 STEP = 64
+PIVOTS = 8
 NT = (((1,), (1,)), ((), ()))
 NN = (((1,), (0,)), ((), ()))
 OFFSETS = sorted(
@@ -318,64 +319,74 @@
     load_rb.start()
     highest = lax.Precision.HIGHEST
 
-    work_a, work_r = [], []
-    for i in range(4):
-        rs = r_ref[pl.ds(4 * i, 4)].reshape(64, 128)
-        middle = lax.dot_general(rs, g_ref[i], NN, precision=highest, preferred_element_type=F32)
-        a = lax.dot_general(middle, rs, NT, precision=highest, preferred_element_type=F32)
-        work_a.append([a[8 * b:8 * b + 8] for b in range(8)])
-        work_r.append([rs[8 * b:8 * b + 8] for b in range(8)])
+    half = 64
+    work = []
+    for pair in range(2):
+        rs = [r_ref[pl.ds(4 * i, 4)].reshape(64, 128) for i in (2 * pair, 2 * pair + 1)]
+        curved = []
+        for n in range(2):
+            middle = lax.dot_general(rs[n], g_ref[2 * pair + n], NN, precision=highest, preferred_element_type=F32)
+            curved.append(lax.dot_general(middle, rs[n], NT, precision=highest, preferred_element_type=F32))
+        parts = (
+            jnp.concatenate(curved, axis=1),
+            jnp.concatenate([rs[0][:, :half], rs[1][:, :half]], axis=1),
+            jnp.concatenate([rs[0][:, half:], rs[1][:, half:]], axis=1),
+        )
+        work.append([[part[8 * b:8 * b + 8] for b in range(8)] for part in parts])
 
     sub = lax.broadcasted_iota(jnp.int32, (8, 128), 0)
-    for step in range(16):
-        b, o = divmod(4 * step, 8)
-        for i in range(4):
-            a, rr = work_a[i], work_r[i]
-            cols = [
-                [jnp.broadcast_to(a[n][:, 4 * step + p:4 * step + p + 1], (8, 128)) for n in range(b, 8)]
-                for p in range(4)
-            ]
-            ra = [a[b][o + p:o + p + 1] for p in range(4)]
-            rw = [rr[b][o + p:o + p + 1] for p in range(4)]
-            mult, ua, ur = [], [], []
-            for p in range(4):
-                col, va, vr = cols[p], ra[p], rw[p]
+    left = lax.broadcasted_iota(jnp.int32, (8, 128), 1) < half
+    for step in range(64 // PIVOTS):
+        b, o = divmod(PIVOTS * step, 8)
+        below = sub >= o + PIVOTS
+        for parts in work:
+            a = parts[0]
+            mult, rows = [], []
+            for p in range(PIVOTS):
+                k = PIVOTS * step + p
+                col = [
+                    jnp.take_along_axis(a[n], jnp.where(left, k, half + k), axis=1, mode="promise_in_bounds")
+                    for n in range(b, 8)
+                ]
+                row = [part[b][o + p:o + p + 1] for part in parts]
                 for q in range(p):
                     l = mult[q][0][o + p:o + p + 1]
                     col = [cc - mm * l for cc, mm in zip(col, mult[q])]
-                    va = va - l[:, :64] * ua[q]
-                    vr = vr - l * ur[q]
+                    row = [rr - l * uu for rr, uu in zip(row, rows[q])]
                 inv = lax.rsqrt(col[0][o + p:o + p + 1])
                 mult.append([cc * inv for cc in col])
-                ua.append(va * inv[:, :64])
-                ur.append(vr * inv)
-            below = sub >= o + 4
-            for n in range(b, 8):
-                if n == b and o == 4:
-                    continue
-                da = sum(mult[p][n - b][:, :64] * ua[p] for p in range(4))
-                dr = sum(mult[p][n - b] * ur[p] for p in range(4))
-                if n == b:
-                    da = jnp.where(below[:, :64], da, 0.0)
-                    dr = jnp.where(below, dr, 0.0)
-                a[n] = a[n] - da
-                rr[n] = rr[n] - dr
-            fin = rr[b]
-            for p in range(4):
-                fin = jnp.where(sub == o + p, ur[p], fin)
-            rr[b] = fin
+                rows.append([rr * inv for rr in row])
+            for m, part in enumerate(parts):
+                for n in range(b, 8):
+                    if n == b and o + PIVOTS == 8:
+                        continue
+                    delta = sum(mult[p][n - b] * rows[p][m] for p in range(PIVOTS))
+                    if n == b:
+                        delta = jnp.where(below, delta, 0.0)
+                    part[n] = part[n] - delta
+                if m:
+                    done = part[b]
+                    for p in range(PIVOTS):
+                        done = jnp.where(sub == o + p, rows[p][m], done)
+                    part[b] = done
 
     load_rb.wait()
     for i in range(4):
-        coeff = jnp.concatenate(work_r[i], axis=0)
+        lanes = slice(half * (i % 2), half * (i % 2) + half)
+        coeff = jnp.concatenate(
+            [jnp.concatenate(work[i // 2][m], axis=0)[:, lanes] for m in (1, 2)], axis=1
+        )
         hi, lo = split_hi_lo(coeff)
-        basis = rbv[i]
-        nb[i] = (
-            lax.dot_general(hi, basis, NN, preferred_element_type=F32)
-            + lax.dot_general(lo, basis, NN, preferred_element_type=F32)
-        )
-        p = lax.dot_general(coeff, g_ref[i], NN, precision=highest, preferred_element_type=F32)
-        hi, lo = split_hi_lo(p)
+        gram_hi, gram_lo = split_hi_lo(g_ref[i])
+        both = lax.dot_general(
+            jnp.concatenate([hi, lo], axis=0),
+            jnp.concatenate([rbv[i], gram_hi], axis=1),
+            NN,
+            preferred_element_type=F32,
+        )
+        both = both[:64] + both[64:]
+        nb[i] = both[:, :128]
+        hi, lo = split_hi_lo(both[:, 128:] + lax.dot_general(hi, gram_lo, NN, preferred_element_type=F32))
         proj[i] = jnp.concatenate([hi, lo], axis=0)
 
     load_cp.wait()

time: 48.3 us -> 47.8 us (0.990)
  Pallas kernels: 47.6 us -> 47 us
    pallas_call x1, Pallas kernels: 6.76 us -> 6.21 us  [back(): pl.pallas_call(back_kernel, out_shape=(jax.ShapeDtypeStruct((4, 64, 128),...]
where the time goes in v5:
time: 47.8 us; the launch traced here: 47.7 us
  Pallas kernels  47 us (98%)
  between operations  0.64 us (1%)
    pallas_call x1, Pallas kernels, front(): pl.pallas_call(front_kernel, out_shape=(pltpu.VMEM((NCOL, 16, 128), F32),...  40.8 us
    pallas_call x1, Pallas kernels, back(): pl.pallas_call(back_kernel, out_shape=(jax.ShapeDtypeStruct((4, 64, 128),...  6.21 us

profile of v5, /device:TPU:0, one launch (start us, length us, event | category | flops | bytes accessed | tf_op | source)
XLA Modules:
  0.0 47.7 jit_solution(17360377756296273936)
XLA Ops:
  0.6 40.8 %shard_map.77 = (f32[16,16,128]{2,1,0:T(8,128)S(1)}, f32[4,128,128]{2,1,0:T(8,128)S(1)}) custom-call(bf16[48,128,256]{2,1,0:T(8,128)(2,1)} %cb.1, bf16[48,64,256]{2,1,0:T(8,128)(2,1)} %tm.1, bf16[64,64,128]{2,1,0:T(8,128)(2,1)} %cp.3, bf16[4,128,128]{2,1,0:T(8,128)(2,1)} %rb.3, s32[1,64]{1,0:T(1,128)} %bitcast.3, s32[1,64]{1,0:T(1,128)} %bitcast.2), custom_call_target="tpu_custom_call" | custom-call | tf_op jit(solution)/shard_map/pallas_call | solution.py:275
  41.4 6.2 %shard_map.78 = (f32[4,64,128]{2,1,0:T(8,128)}, f32[64,64,128]{2,1,0:T(8,128)}) custom-call(s32[64]{0:T(128)} %rows_s.1, f32[16,16,128]{2,1,0:T(8,128)S(1)} %get-tuple-element.4.r_ref, f32[4,128,128]{2,1,0:T(8,128)S(1)} %get-tuple-element.5.g_ref, bf16[4,128,128]{2,1,0:T(8,128)(2,1)} %rb.3, bf16[64,64,128]{2,1,0:T(8,128)(2,1)} %cp.3), custom_call_target="tpu_custom_call" | custom-call | tf_op jit(solution)/shard_map/pallas_call | solution.py:414

commit v6 on v5

--- a/solution.py
+++ b/solution.py
@@ -105,6 +105,10 @@
             src_ref=src, dst_ref=dst, send_sem=send, recv_sem=recv, device_id=device, device_id_type=MESH
         )
 
+    def all_of(ref, sem):
+        pltpu.make_async_copy(ref, ref, sem).wait()
+
+    others = pl.ds(0, len(OFFSETS))
     started = []
 
     def go(copy):
@@ -123,18 +127,12 @@
     for m, (s, q) in enumerate(order):
         at = pl.ds(piece(s, q), HC)
         to_partner[s, q] = go(remote(part.at[at], prx.at[at], pc_send.at[m], pc_recv.at[m], partner))
-    labels = [
-        go(remote(idxv.at[k], idxv.at[k], ix_send.at[n], ix_recv.at[n], (r, c)))
-        for n, c in enumerate(peers)
-    ]
-    gram1 = [
-        go(remote(gpart.at[pl.ds(8 * c, 8)], grx.at[n], g1_send.at[n], g1_recv.at[n], (r, c)))
-        for n, c in enumerate(peers)
-    ]
-    moves = [
-        go(remote(cp.at[pl.ds(4 * c, 4)], cpl.at[k], cp_send.at[n], cp_recv.at[n], (r, c)))
-        for n, c in enumerate(peers)
-    ]
+    for n, c in enumerate(peers):
+        remote(idxv.at[k], idxv.at[k], ix_send, ix_recv, (r, c)).start()
+    for n, c in enumerate(peers):
+        remote(gpart.at[pl.ds(8 * c, 8)], grx.at[n], g1_send, g1_recv, (r, c)).start()
+    for n, c in enumerate(peers):
+        remote(cp.at[pl.ds(4 * c, 4)], cpl.at[k], cp_send, cp_recv, (r, c)).start()
 
     scatter = {}
     for s, q in order:
@@ -184,16 +182,13 @@
             gather[s, q] = spread(mine, ag_send, ag_recv, 3 * s + q - 1, along[q])
         forwarded.append((s, 0, spread(mine, fw_send, fw_recv, 4 * s, partner)))
         rests(mine)
-    for copy in gram1:
-        copy.wait_recv()
+    all_of(grx, g1_recv)
     total = gpart[pl.ds(pl.multiple_of(8 * k, 8), 8)]
     for n in range(len(OFFSETS)):
         total = total + grx[n]
     gall[k] = total
-    gram2 = [
-        go(remote(gall.at[k], gall.at[k], g2_send.at[n], g2_recv.at[n], (r, c)))
-        for n, c in enumerate(peers)
-    ]
+    for n, c in enumerate(peers):
+        remote(gall.at[k], gall.at[k], g2_send, g2_recv, (r, c)).start()
 
     for s in range(SUBS):
         for q in (1, 3, 2):
@@ -203,10 +198,8 @@
             rests(start)
 
     own_cp.wait()
-    for copy in labels:
-        copy.wait_recv()
-    for copy in moves:
-        copy.wait_recv()
+    all_of(idxv.at[others], ix_recv)
+    all_of(cpl.at[others], cp_recv)
     to_scalars = pltpu.make_async_copy(idxv, idxs, misc_sem.at[2])
     to_scalars.start()
     first = lax.broadcasted_iota(jnp.int32, (64, 128), 1) < 64
@@ -241,30 +234,29 @@
     for i in range(4):
         rpart[pl.ds(4 * i, 4)] = sums[i].reshape(4, 16, 128)
 
-    row1 = [
-        go(remote(rpart.at[c], rrx.at[n], r1_send.at[n], r1_recv.at[n], (r, c)))
-        for n, c in enumerate(peers)
-    ]
-    for copy in gram2:
-        copy.wait_recv()
+    for n, c in enumerate(peers):
+        remote(rpart.at[c], rrx.at[n], r1_send, r1_recv, (r, c)).start()
+    all_of(gall.at[others], g2_recv)
     for c in range(NCOL):
         for i in range(4):
             out_g[i, pl.ds(8 * c, 8)] = gall[c, :, pl.ds(128 * i, 128)]
-    for copy in row1:
-        copy.wait_recv()
+    for copy in started:
+        copy.wait_send()
+    all_of(idxv.at[others], ix_send)
+    all_of(cpl.at[others], cp_send)
+    all_of(grx, g1_send)
+    all_of(gall.at[others], g2_send)
+    all_of(rrx, r1_recv)
     total = rpart[k]
     for n in range(len(OFFSETS)):
         total = total + rrx[n]
     rall[k] = total
-    row2 = [
-        go(remote(rall.at[k], rall.at[k], r2_send.at[n], r2_recv.at[n], (r, c)))
-        for n, c in enumerate(peers)
-    ]
-    for copy in row2:
-        copy.wait_recv()
+    for n, c in enumerate(peers):
+        remote(rall.at[k], rall.at[k], r2_send, r2_recv, (r, c)).start()
+    all_of(rrx, r1_send)
+    all_of(rall.at[others], r2_recv)
     out_r[...] = rall[...]
-    for copy in started:
-        copy.wait_send()
+    all_of(rall.at[others], r2_send)
 
 
 def front(cb, tm, cp, rb, tcols, trows):
@@ -305,7 +297,7 @@
             pltpu.VMEM((NCOL, 16, 128), F32),
             dma((2, 8 * SUBS)), dma((3,)),
             dma((4 * SUBS,)), dma((4 * SUBS,)),
-        ] + [dma((6 * SUBS,))] * 4 + [dma((8 * SUBS,))] * 2 + [dma((peers,))] * 12,
+        ] + [dma((6 * SUBS,))] * 4 + [dma((8 * SUBS,))] * 2 + [dma] * 12,
         compiler_params=pltpu.CompilerParams(
             collective_id=0, has_side_effects=True, vmem_limit_bytes=60 * 1024 * 1024
         ),

time: 47.8 us -> 46 us (0.962)
  Pallas kernels: 47 us -> 45.3 us
    pallas_call x1, Pallas kernels: 40.8 us -> 39.1 us  [front(): pl.pallas_call(front_kernel, out_shape=(pltpu.VMEM((NCOL, 16, 128), F32),...]
where the time goes in v6:
time: 46 us; the launch traced here: 45.9 us
  Pallas kernels  45.3 us (98%)
  between operations  0.64 us (1%)
    pallas_call x1, Pallas kernels, front(): pl.pallas_call(front_kernel, out_shape=(pltpu.VMEM((NCOL, 16, 128), F32),...  39.1 us
    pallas_call x1, Pallas kernels, back(): pl.pallas_call(back_kernel, out_shape=(jax.ShapeDtypeStruct((4, 64, 128),...  6.21 us

profile of v6, /device:TPU:0, one launch (start us, length us, event | category | flops | bytes accessed | tf_op | source)
XLA Modules:
  0.0 45.9 jit_solution(1752490905874378621)
XLA Ops:
  0.6 39.1 %shard_map.77 = (f32[16,16,128]{2,1,0:T(8,128)S(1)}, f32[4,128,128]{2,1,0:T(8,128)S(1)}) custom-call(bf16[48,128,256]{2,1,0:T(8,128)(2,1)} %cb.1, bf16[48,64,256]{2,1,0:T(8,128)(2,1)} %tm.1, bf16[64,64,128]{2,1,0:T(8,128)(2,1)} %cp.3, bf16[4,128,128]{2,1,0:T(8,128)(2,1)} %rb.3, s32[1,64]{1,0:T(1,128)} %bitcast.3, s32[1,64]{1,0:T(1,128)} %bitcast.2), custom_call_target="tpu_custom_call" | custom-call | tf_op jit(solution)/shard_map/pallas_call | solution.py:267
  39.7 6.2 %shard_map.78 = (f32[4,64,128]{2,1,0:T(8,128)}, f32[64,64,128]{2,1,0:T(8,128)}) custom-call(s32[64]{0:T(128)} %rows_s.1, f32[16,16,128]{2,1,0:T(8,128)S(1)} %get-tuple-element.4.r_ref, f32[4,128,128]{2,1,0:T(8,128)S(1)} %get-tuple-element.5.g_ref, bf16[4,128,128]{2,1,0:T(8,128)(2,1)} %rb.3, bf16[64,64,128]{2,1,0:T(8,128)(2,1)} %cp.3), custom_call_target="tpu_custom_call" | custom-call | tf_op jit(solution)/shard_map/pallas_call | solution.py:406

commit v7 on v6

--- a/solution.py
+++ b/solution.py
@@ -74,13 +74,13 @@
     order = [(s, q) for s in range(SUBS) for q in (2, 1, 3, 0)]
     loads = {}
     for n, half in enumerate((1 - h, h)):
-        for m, (s, q) in enumerate(order):
-            at = pl.ds(half * HALF + piece(s, q), HC)
-            a = pltpu.make_async_copy(cb.at[at], cbv.at[at], ld_sem.at[0, 4 * SUBS * n + m])
-            b = pltpu.make_async_copy(tm.at[at], tmv.at[at], ld_sem.at[1, 4 * SUBS * n + m])
+        for m, q in enumerate((2, 1, 3, 0)):
+            at = pl.ds(half * HALF + piece(0, q), CH)
+            a = pltpu.make_async_copy(cb.at[at], cbv.at[at], ld_sem.at[0, 4 * n + m])
+            b = pltpu.make_async_copy(tm.at[at], tmv.at[at], ld_sem.at[1, 4 * n + m])
             a.start()
             b.start()
-            loads[n, s, q] = (a, b)
+            loads[n, q] = (a, b)
     load_rb = pltpu.make_async_copy(rb, rbv, misc_sem.at[0])
     load_rb.start()
     own_cp = pltpu.make_async_copy(cp.at[pl.ds(4 * k, 4)], cpl.at[k], misc_sem.at[1])
@@ -91,7 +91,7 @@
         pl.semaphore_signal(barrier, inc=1, device_id=device, device_id_type=MESH)
 
     def sketch(n, s, q, dst):
-        for load in loads[n, s, q]:
+        for load in loads[n, q] if s == 0 else ():
             load.wait()
         half = (1 - h) if n == 0 else h
         base = half * HALF + piece(s, q)
@@ -134,7 +134,6 @@
     for n, c in enumerate(peers):
         remote(cp.at[pl.ds(4 * c, 4)], cpl.at[k], cp_send, cp_recv, (r, c)).start()
 
-    scatter = {}
     for s, q in order:
         sketch(1, s, q, own)
         to_partner[s, q].wait_recv()
@@ -145,18 +144,16 @@
         n = 3 * s + q - 1
         for u in range(HC):
             zsh[n, u], zsw[n, u] = code(own[at + u] + prx[at + u])
-        scatter[s, q] = (
-            go(remote(zsh.at[n], zrh.at[n], zs_send.at[2 * n], zs_recv.at[2 * n], along[q])),
-            go(remote(zsw.at[n], zrw.at[n], zs_send.at[2 * n + 1], zs_recv.at[2 * n + 1], along[q])),
-        )
-
-
-    def spread(start, send, recv, n, device):
+        go(remote(zsh.at[n], zrh.at[n], zs_send.at[2 * n], zs_recv.at[2 * s], along[q]))
+        go(remote(zsw.at[n], zrw.at[n], zs_send.at[2 * n + 1], zs_recv.at[2 * s + 1], along[q]))
+
+
+    def spread(start, send, recv, n, m, device):
         heads = skb.at[pl.ds(start, HC), pl.ds(0, 64)]
         words = skw.at[pl.ds(start, HC)]
         return (
-            go(remote(heads, heads, send.at[2 * n], recv.at[2 * n], device)),
-            go(remote(words, words, send.at[2 * n + 1], recv.at[2 * n + 1], device)),
+            go(remote(heads, heads, send.at[2 * n], recv.at[2 * m], device)),
+            go(remote(words, words, send.at[2 * n + 1], recv.at[2 * m + 1], device)),
         )
 
     def arrived(copies):
@@ -167,10 +164,10 @@
         for u in range(HC):
             skb[start + u, 64:] = rest_of(skb[start + u, :64], skw[start + u]).astype(BF16)
 
-    gather, forwarded = {}, []
+    gather = {}
     for s in range(SUBS):
-        for q in (1, 2, 3):
-            arrived(scatter[s, q])
+        all_of(zrh.at[pl.ds(3 * s, 3)], zs_recv.at[2 * s])
+        all_of(zrw.at[pl.ds(3 * s, 3)], zs_recv.at[2 * s + 1])
         mine = h * HALF + piece(s, 0)
         for u in range(HC):
             total = own[piece(s, 0) + u]
@@ -179,8 +176,8 @@
                 total = total + (head.astype(F32) + rest_of(head, zrw[n, u]))
             skb[mine + u, :64], skw[mine + u] = code(total)
         for q in (2, 1, 3):
-            gather[s, q] = spread(mine, ag_send, ag_recv, 3 * s + q - 1, along[q])
-        forwarded.append((s, 0, spread(mine, fw_send, fw_recv, 4 * s, partner)))
+            gather[s, q] = spread(mine, ag_send, ag_recv, 3 * s + q - 1, 3 * s + q - 1, along[q])
+        spread(mine, fw_send, fw_recv, 4 * s, 0, partner)
         rests(mine)
     all_of(grx, g1_recv)
     total = gpart[pl.ds(pl.multiple_of(8 * k, 8), 8)]
@@ -194,7 +191,7 @@
         for q in (1, 3, 2):
             arrived(gather[s, q])
             start = h * HALF + piece(s, 4 - q)
-            forwarded.append((s, 4 - q, spread(start, fw_send, fw_recv, 4 * s + q, partner)))
+            spread(start, fw_send, fw_recv, 4 * s + q, 0, partner)
             rests(start)
 
     own_cp.wait()
@@ -214,8 +211,9 @@
             ).astype(BF16)
 
     to_scalars.wait()
-    for s, q, copies in forwarded:
-        arrived(copies)
+    all_of(skb.at[pl.ds(0, HALF), pl.ds(0, 64)], fw_recv.at[0])
+    all_of(skw.at[pl.ds(0, HALF)], fw_recv.at[1])
+    for s, q in order:
         rests((1 - h) * HALF + piece(s, q))
 
     def tiles(n, carry):
@@ -295,7 +293,7 @@
             pltpu.VMEM((NCOL, 16, 128), F32),
             pltpu.VMEM((peers, 16, 128), F32),
             pltpu.VMEM((NCOL, 16, 128), F32),
-            dma((2, 8 * SUBS)), dma((3,)),
+            dma((2, 8)), dma((3,)),
             dma((4 * SUBS,)), dma((4 * SUBS,)),
         ] + [dma((6 * SUBS,))] * 4 + [dma((8 * SUBS,))] * 2 + [dma] * 12,
         compiler_params=pltpu.CompilerParams(

time: 46 us -> 46 us (level)
  no operation moved by 1% of the time
where the time goes in v7:
time: 46 us; the launch traced here: 45.9 us
  Pallas kernels  45.2 us (98%)
  between operations  0.64 us (1%)
    pallas_call x1, Pallas kernels, front(): pl.pallas_call(front_kernel, out_shape=(pltpu.VMEM((NCOL, 16, 128), F32),...  39 us
    pallas_call x1, Pallas kernels, back(): pl.pallas_call(back_kernel, out_shape=(jax.ShapeDtypeStruct((4, 64, 128),...  6.21 us

profile of v7, /device:TPU:0, one launch (start us, length us, event | category | flops | bytes accessed | tf_op | source)
XLA Modules:
  0.0 45.9 jit_solution(9084440520520455707)
XLA Ops:
  0.6 39.0 %shard_map.77 = (f32[16,16,128]{2,1,0:T(8,128)S(1)}, f32[4,128,128]{2,1,0:T(8,128)S(1)}) custom-call(bf16[48,128,256]{2,1,0:T(8,128)(2,1)} %cb.1, bf16[48,64,256]{2,1,0:T(8,128)(2,1)} %tm.1, bf16[64,64,128]{2,1,0:T(8,128)(2,1)} %cp.3, bf16[4,128,128]{2,1,0:T(8,128)(2,1)} %rb.3, s32[1,64]{1,0:T(1,128)} %bitcast.3, s32[1,64]{1,0:T(1,128)} %bitcast.2), custom_call_target="tpu_custom_call" | custom-call | tf_op jit(solution)/shard_map/pallas_call | solution.py:265
  39.7 6.2 %shard_map.78 = (f32[4,64,128]{2,1,0:T(8,128)}, f32[64,64,128]{2,1,0:T(8,128)}) custom-call(s32[64]{0:T(128)} %rows_s.1, f32[16,16,128]{2,1,0:T(8,128)S(1)} %get-tuple-element.4.r_ref, f32[4,128,128]{2,1,0:T(8,128)S(1)} %get-tuple-element.5.g_ref, bf16[4,128,128]{2,1,0:T(8,128)(2,1)} %rb.3, bf16[64,64,128]{2,1,0:T(8,128)(2,1)} %cp.3), custom_call_target="tpu_custom_call" | custom-call | tf_op jit(solution)/shard_map/pallas_call | solution.py:404
